TPU v7x, 32 devices: a whole 2x2x4 slice. The times are simulated.
32 devices in a mesh: ctx: 8 (over z, x), head: 4 (over y, core).
Axes of the slice: x: 2, y: 2, z: 4, core: 2. Of those that a mesh axis runs over, the one named last changes fastest.
Arguments:
- queries: bfloat16 [2048, 64, 128], P('ctx', 'head'), may hold values from -16 to 16
- keys: bfloat16 [2048, 8, 128], P(('ctx', 'head')), may hold values from -8 to 8
- values: bfloat16 [2048, 8, 128], P(('ctx', 'head')), may hold values from -6 to 6
- grad_out: bfloat16 [2048, 64, 128], P('ctx', 'head'), may hold values from -6 to 6
- lengths: int32 [8], replicated, may hold values from 1 to 768, 2048 in all
Outputs:
- attended: bfloat16 [2048, 64, 128], P('ctx', 'head')
- d_queries: bfloat16 [2048, 64, 128], P('ctx', 'head')
- d_keys: bfloat16 [2048, 8, 128], P(('ctx', 'head'))
- d_values: bfloat16 [2048, 8, 128], P(('ctx', 'head'))
Inputs may be any that keep to these rules, and one draw needn't show every extreme that they name: `lengths`: the 8 documents fill the window; the longest has exactly 768 tokens.
All inputs are finite; a program needn't handle non-finite values.
Results may differ from a plain program's by a relative error of at most 0.0085.
Values may be sent and summed in bfloat16 or wider, within the bound.
No kernel may reach another device: no remote copies, remote signals or barrier semaphores. Data moves between devices by JAX's collectives and lax.ppermute only.
A program may use at most 64 MiB of HBM per device.

v0:
```python
import jax
import jax.numpy as jnp
from jax import lax
from jax.sharding import PartitionSpec as P

BACK = 3


def shifted(block, axis, distance):
    devices = range(lax.axis_size(axis))
    route = [(i - distance, i) for i in devices if i - distance in devices]
    return lax.ppermute(block, axis, route)


def head_pass(query_rows, grad_rows, key_rows, value_rows, allowed):
    inv_root = query_rows.shape[-1] ** (-0.5)
    scores = jnp.dot(query_rows, key_rows.T, preferred_element_type=jnp.float32) * inv_root
    masked = jnp.where(allowed, scores, -jnp.inf)
    top_score = jnp.max(masked, axis=1, keepdims=True)
    log_total = top_score + jnp.log(jnp.sum(jnp.exp(masked - top_score), axis=1, keepdims=True))
    probs = jnp.exp(masked - log_total)
    probs_low = probs.astype(jnp.bfloat16)
    attended = jnp.dot(probs_low, value_rows, preferred_element_type=jnp.float32).astype(
        jnp.bfloat16
    )
    correction = jnp.sum(
        grad_rows.astype(jnp.float32) * attended.astype(jnp.float32), axis=1, keepdims=True
    )
    grad_probs = jnp.dot(grad_rows, value_rows.T, preferred_element_type=jnp.float32)
    grad_scores = (probs * (grad_probs - correction)).astype(jnp.bfloat16)
    grad_values = jnp.dot(probs_low.T, grad_rows, preferred_element_type=jnp.float32)
    grad_query = (
        jnp.dot(grad_scores, key_rows, preferred_element_type=jnp.float32) * inv_root
    ).astype(jnp.bfloat16)
    grad_keys = jnp.dot(grad_scores.T, query_rows, preferred_element_type=jnp.float32) * inv_root
    return (attended, grad_query, grad_keys, grad_values, log_total, correction)


def group_pass(query_group, grad_group, key_rows, value_rows, allowed):

    def one_head(head_inputs):
        return head_pass(head_inputs[0], head_inputs[1], key_rows, value_rows, allowed)

    attended, grad_query, grad_keys, grad_values, log_total, correction = lax.map(
        one_head, (jnp.moveaxis(query_group, 1, 0), jnp.moveaxis(grad_group, 1, 0))
    )
    return (
        jnp.moveaxis(attended, 0, 1),
        jnp.moveaxis(grad_query, 0, 1),
        jnp.sum(grad_keys, axis=0),
        jnp.sum(grad_values, axis=0),
        jnp.moveaxis(log_total[:, :, 0], 0, 1),
        jnp.moveaxis(correction[:, :, 0], 0, 1),
    )


def attend(query_split, grad_split, key_span, value_span, allowed):
    results = [
        group_pass(
            query_split[:, group],
            grad_split[:, group],
            key_span[:, group],
            value_span[:, group],
            allowed,
        )
        for group in range(query_split.shape[1])
    ]
    return tuple(
        (jnp.stack([member[slot_index] for member in results], axis=1) for slot_index in range(6))
    )


def on_device(queries, keys, values, grad_out, lengths):
    key_local, value_local = (
        lax.all_to_all(keys, "head", split_axis=1, concat_axis=0, tiled=True),
        lax.all_to_all(values, "head", split_axis=1, concat_axis=0, tiled=True),
    )
    tok_dev = queries.shape[0]
    groups = key_local.shape[1]
    head_dim = queries.shape[2]
    per_group = queries.shape[1] // groups
    query_split = queries.reshape(tok_dev, groups, per_group, head_dim)
    grad_split = grad_out.reshape(tok_dev, groups, per_group, head_dim)
    shard = lax.axis_index("ctx")
    query_pos = shard * tok_dev + jnp.arange(tok_dev, dtype=jnp.int32)
    starts = jnp.cumsum(lengths) - lengths
    query_start = jnp.max(
        jnp.where(starts[None, :] <= query_pos[:, None], starts[None, :], 0), axis=1
    )
    near_key, near_value = shifted((key_local, value_local), "ctx", 1)
    far_pair = shifted((key_local, value_local, near_key, near_value), "ctx", 2)
    key_span = jnp.concatenate([far_pair[2], far_pair[0], near_key, key_local], axis=0)
    value_span = jnp.concatenate([far_pair[3], far_pair[1], near_value, value_local], axis=0)
    key_pos = (shard - BACK) * tok_dev + jnp.arange((BACK + 1) * tok_dev, dtype=jnp.int32)
    allowed = (key_pos[None, :] >= query_start[:, None]) & (key_pos[None, :] <= query_pos[:, None])
    attended, grad_query, grad_keys, grad_values, log_total, correction = attend(
        query_split, grad_split, key_span, value_span, allowed
    )
    key_blocks = grad_keys.reshape(BACK + 1, tok_dev, groups, head_dim)
    value_blocks = grad_values.reshape(BACK + 1, tok_dev, groups, head_dim)
    far_back = shifted((key_blocks[1], value_blocks[1], key_blocks[0], value_blocks[0]), "ctx", -2)
    near_back = shifted((key_blocks[2] + far_back[2], value_blocks[2] + far_back[3]), "ctx", -1)
    key_total = key_blocks[3] + far_back[0] + near_back[0]
    value_total = value_blocks[3] + far_back[1] + near_back[1]
    d_keys, d_values = (
        lax.all_to_all(
            key_total.astype(jnp.bfloat16), "head", split_axis=0, concat_axis=1, tiled=True
        ),
        lax.all_to_all(
            value_total.astype(jnp.bfloat16), "head", split_axis=0, concat_axis=1, tiled=True
        ),
    )
    return (
        attended.reshape(tok_dev, groups * per_group, head_dim),
        grad_query.reshape(tok_dev, groups * per_group, head_dim),
        d_keys,
        d_values,
    )


def solution(mesh):
    placed = (
        P("ctx", "head", None),
        P(("ctx", "head"), None, None),
        P(("ctx", "head"), None, None),
        P("ctx", "head", None),
        P(),
    )
    return jax.shard_map(
        on_device,
        mesh=mesh,
        in_specs=placed,
        out_specs=(
            P("ctx", "head", None),
            P("ctx", "head", None),
            P(("ctx", "head"), None, None),
            P(("ctx", "head"), None, None),
        ),
        check_vma=False,
    )
```

profile of v0, /device:TPU:18, one launch (start us, length us, event | category | flops | bytes accessed | tf_op | source)
XLA Modules:
  0.0 201.9 jit_solution(18116497599587120612)
XLA Ops:
  2.3 3.3 %all-to-all-start = ((bf16[64,8,128]{2,0,1:T(8,128)(2,1)}), bf16[64,8,128]{2,0,1:T(8,128)(2,1)S(1)}, u32[]{:S(2)}, u32[]{:S(2)}) async-start(bf16[64,8,128]{2,0,1:T(8,128)(2,1)} %copy.54), calls=%async_computation | async-start | bytes 262144 | tf_op jit(solution)/shard_map/all_to_all | solution.py:75
  10.2 3.3 %all-to-all-start.1 = ((bf16[64,8,128]{2,0,1:T(8,128)(2,1)}), bf16[64,8,128]{2,0,1:T(8,128)(2,1)S(1)}, u32[]{:S(2)}, u32[]{:S(2)}) async-start(bf16[64,8,128]{2,0,1:T(8,128)(2,1)} %copy.56), calls=%async_computation.1 | async-start | bytes 262144 | tf_op jit(solution)/shard_map/all_to_all | solution.py:76
  13.6 3.5 %collective-permute-start = (bf16[256,2,128]{2,0,1:T(8,128)(2,1)S(1)}, bf16[256,2,128]{2,0,1:T(8,128)(2,1)S(1)}, u32[]{:S(2)}, u32[]{:S(2)}) collective-permute-start(bf16[256,2,128]{2,0,1:T(8,128)(2,1)S(1)} %bitcast.217), channel_id=1, source_target_pairs={{0,4},{4,8},{8,12},{12,16},{16,20},{20,24},{24,28},{1,5},{5,9},{9,... | collective-permute-start | bytes 393224 | tf_op jit(solution)/shard_map/ppermute | solution.py:12
  19.0 2.8 %collective-permute-start.3 = (bf16[256,2,128]{2,0,1:T(8,128)(2,1)S(1)}, bf16[256,2,128]{2,0,1:T(8,128)(2,1)S(1)}, u32[]{:S(2)}, u32[]{:S(2)}) collective-permute-start(bf16[256,2,128]{2,0,1:T(8,128)(2,1)S(1)} %bitcast.220), channel_id=1, source_target_pairs={{0,4},{4,8},{8,12},{12,16},{16,20},{20,24},{24,28},{1,5},{5,9},{9,... | collective-permute-start | bytes 393224 | tf_op jit(solution)/shard_map/ppermute | solution.py:12
  21.8 3.0 %collective-permute-start.1 = (bf16[256,2,128]{2,0,1:T(8,128)(2,1)S(1)}, bf16[256,2,128]{2,0,1:T(8,128)(2,1)S(1)}, u32[]{:S(2)}, u32[]{:S(2)}) collective-permute-start(bf16[256,2,128]{2,0,1:T(8,128)(2,1)S(1)} %collective-permute-done), channel_id=1, source_target_pairs={{0,8},{4,12},{8,16},{12,20},{16,24},{20,28},{1,9},{5,13},{9,17},{1... | collective-permute-start | bytes 393224 | tf_op jit(solution)/shard_map/ppermute | solution.py:12
  28.8 2.6 %collective-permute-done.1 = bf16[256,2,128]{2,0,1:T(8,128)(2,1)S(1)} collective-permute-done((bf16[256,2,128]{2,0,1:T(8,128)(2,1)S(1)}, bf16[256,2,128]{2,0,1:T(8,128)(2,1)S(1)}, u32[]{:S(2)}, u32[]{:S(2)}) %collective-permute-start.1) | collective-permute-done | bytes 131104 | tf_op jit(solution)/shard_map/ppermute | solution.py:12
  31.5 2.7 %collective-permute-done.5 = bf16[256,2,128]{2,0,1:T(8,128)(2,1)S(1)} collective-permute-done((bf16[256,2,128]{2,0,1:T(8,128)(2,1)S(1)}, bf16[256,2,128]{2,0,1:T(8,128)(2,1)S(1)}, u32[]{:S(2)}, u32[]{:S(2)}) %collective-permute-start.5) | collective-permute-done | bytes 131104 | tf_op jit(solution)/shard_map/ppermute | solution.py:12
  36.2 2.3 %broadcast.39.clone.2 = f32[8,1024,128]{2,1,0:T(8,128)} broadcast(f32[]{:T(128)} %constant.58.clone.1), dimensions={} | broadcast | bytes 4194308 | tf_op jit(solution)/shard_map/broadcast.14
  38.5 2.3 %broadcast.39.clone.3 = f32[8,1024,128]{2,1,0:T(8,128)} broadcast(f32[]{:T(128)} %constant.58.clone.1), dimensions={} | broadcast | bytes 4194308 | tf_op jit(solution)/shard_map/broadcast.14
  40.9 48.2 %while.34 = (s32[]{:T(128)}, bf16[8,256,128]{1,2,0:T(8,128)(2,1)S(1)}, bf16[8,256,128]{2,1,0:T(8,128)(2,1)S(1)}, f32[8,1024,128]{2,1,0:T(8,128)}, f32[8,1024,128...) while((s32[]{:T(128)}, ...), condition=%wide.region_6.7_spmd.clone, body=%wide.region_2.6_spmd.clone.sunk | while | flops 407207424 | bytes 9522829 | solution.py:44
  43.4 2.0 %fusion.119 = f32[8,1024,128]{2,1,0:T(8,128)} fusion(f32[8,1024,128]{2,1,0:T(8,128)} %get-tuple-element.597, s32[]{:T(128)} %get-tuple-element.594, bf16[256,1024]{1,0:T(8,128)(2,1)S(1)} %fusion.117, bf16[8,256,128]{2,1,0:T(8,128)(2,1)} %get-tuple-element.612), kind=kOutput, calls=%fused_computation.11.clone.1 | convolution fusion | flops 67239936 | bytes 1115136 | tf_op jit(solution)/shard_map/while/body/eval_jaxpr/dot_general | solution.py:35
  49.5 2.0 %fusion.119 = f32[8,1024,128]{2,1,0:T(8,128)} fusion(f32[8,1024,128]{2,1,0:T(8,128)} %get-tuple-element.597, s32[]{:T(128)} %get-tuple-element.594, bf16[256,1024]{1,0:T(8,128)(2,1)S(1)} %fusion.117, bf16[8,256,128]{2,1,0:T(8,128)(2,1)} %get-tuple-element.612), kind=kOutput, calls=%fused_computation.11.clone.1 | convolution fusion | flops 67239936 | bytes 1115136 | tf_op jit(solution)/shard_map/while/body/eval_jaxpr/dot_general | solution.py:35
  67.5 2.0 fusion.119
  73.5 2.0 fusion.119
  89.2 2.3 %broadcast.39.clone = f32[8,1024,128]{2,1,0:T(8,128)} broadcast(f32[]{:T(128)} %constant.58.clone.1), dimensions={} | broadcast | bytes 4194308 | tf_op jit(solution)/shard_map/broadcast.14
  91.4 2.3 %broadcast.39.clone.1 = f32[8,1024,128]{2,1,0:T(8,128)} broadcast(f32[]{:T(128)} %constant.58.clone.1), dimensions={} | broadcast | bytes 4194308 | tf_op jit(solution)/shard_map/broadcast.14
  93.9 48.1 %while.35 = (s32[]{:T(128)}, bf16[8,256,128]{1,2,0:T(8,128)(2,1)S(1)}, bf16[8,256,128]{2,1,0:T(8,128)(2,1)S(1)}, f32[8,1024,128]{2,1,0:T(8,128)}, f32[8,1024,128...) while((s32[]{:T(128)}, ...), condition=%wide.region_11.12_spmd.clone, body=%wide.region_7.11_spmd.clone.sunk | while | flops 407207424 | bytes 9522829 | solution.py:44
  114.4 2.0 fusion.134
  126.4 2.0 fusion.134
  138.4 2.0 fusion.134
  142.0 2.4 %reduce_sum.74 = f32[1024,128]{1,0:T(8,128)S(1)} reduce(f32[8,1024,128]{2,1,0:T(8,128)} %get-tuple-element.120, f32[]{:T(128)} %constant.58.clone.1), dimensions={0}, to_apply=%region_14.15 | reduce | flops 917504 | bytes 4718596 | tf_op jit(solution)/shard_map/reduce_sum | solution.py:51
  144.4 2.4 %reduce_sum.75 = f32[1024,128]{1,0:T(8,128)S(1)} reduce(f32[8,1024,128]{2,1,0:T(8,128)} %get-tuple-element.121, f32[]{:T(128)} %constant.58.clone.1), dimensions={0}, to_apply=%region_15.16 | reduce | flops 917504 | bytes 4718596 | tf_op jit(solution)/shard_map/reduce_sum | solution.py:51
  148.2 2.8 %collective-permute-start.10 = (f32[256,2,128]{2,1,0:T(2,128)}, f32[256,2,128]{2,1,0:T(2,128)}, u32[]{:S(2)}, u32[]{:S(2)}) collective-permute-start(f32[256,2,128]{2,1,0:T(2,128)} %get-tuple-element.369), channel_id=1, source_target_pairs={{8,0},{12,4},{16,8},{20,12},{24,16},{28,20},{9,1},{13,5},{17,9},{2... | collective-permute-start | bytes 786440 | tf_op jit(solution)/shard_map/ppermute | solution.py:12
  150.9 2.4 %reduce_sum.72 = f32[1024,128]{1,0:T(8,128)S(1)} reduce(f32[8,1024,128]{2,1,0:T(8,128)} %get-tuple-element.118, f32[]{:T(128)} %constant.58.clone.1), dimensions={0}, to_apply=%region_12.13 | reduce | flops 917504 | bytes 4718596 | tf_op jit(solution)/shard_map/reduce_sum | solution.py:50
  153.4 2.4 %reduce_sum.73 = f32[1024,128]{1,0:T(8,128)S(1)} reduce(f32[8,1024,128]{2,1,0:T(8,128)} %get-tuple-element.119, f32[]{:T(128)} %constant.58.clone.1), dimensions={0}, to_apply=%region_13.14 | reduce | flops 917504 | bytes 4718596 | tf_op jit(solution)/shard_map/reduce_sum | solution.py:50
  163.4 2.5 %collective-permute-start.11 = (f32[256,2,128]{2,1,0:T(2,128)S(1)}, f32[256,2,128]{2,1,0:T(2,128)S(1)}, u32[]{:S(2)}, u32[]{:S(2)}) collective-permute-start(f32[256,2,128]{2,1,0:T(2,128)S(1)} %fusion.61), channel_id=1, source_target_pairs={{4,0},{8,4},{12,8},{16,12},{20,16},{24,20},{28,24},{5,1},{9,5},{13... | collective-permute-start | bytes 786440 | tf_op jit(solution)/shard_map/ppermute | solution.py:12
  168.5 2.7 %collective-permute-start.8 = (f32[256,2,128]{2,1,0:T(2,128)}, f32[256,2,128]{2,1,0:T(2,128)}, u32[]{:S(2)}, u32[]{:S(2)}) collective-permute-start(f32[256,2,128]{2,1,0:T(2,128)} %fusion.59), channel_id=1, source_target_pairs={{4,0},{8,4},{12,8},{16,12},{20,16},{24,20},{28,24},{5,1},{9,5},{13... | collective-permute-start | bytes 786440 | tf_op jit(solution)/shard_map/ppermute | solution.py:12
  173.1 11.1 %collective-permute-done.11 = f32[256,2,128]{2,1,0:T(2,128)S(1)} collective-permute-done((f32[256,2,128]{2,1,0:T(2,128)S(1)}, f32[256,2,128]{2,1,0:T(2,128)S(1)}, u32[]{:S(2)}, u32[]{:S(2)}) %collective-permute-start.11) | collective-permute-done | bytes 262176 | tf_op jit(solution)/shard_map/ppermute | solution.py:12
  185.2 3.3 %all-to-all-start.3 = ((bf16[256,2,128]{2,1,0:T(2,128)(2,1)}), bf16[256,2,128]{2,1,0:T(2,128)(2,1)S(1)}, u32[]{:S(2)}, u32[]{:S(2)}) async-start(bf16[256,2,128]{2,1,0:T(2,128)(2,1)} %add_convert_fusion), calls=%async_computation.3 | async-start | bytes 262144 | tf_op jit(solution)/shard_map/all_to_all | solution.py:109
  188.6 2.0 add_convert_fusion.1
  190.6 2.6 %all-to-all-done.3 = bf16[256,2,128]{2,1,0:T(2,128)(2,1)S(1)} async-done(((bf16[256,2,128]{2,1,0:T(2,128)(2,1)}), bf16[256,2,128]{2,1,0:T(2,128)(2,1)S(1)}, u32[]{:S(2)}, u32[]{:S(2)}) %all-to-all-start.3) | async-done | bytes 131104 | tf_op jit(solution)/shard_map/all_to_all | solution.py:109
  193.1 3.3 %all-to-all-start.2 = ((bf16[256,2,128]{2,1,0:T(2,128)(2,1)}), bf16[256,2,128]{2,1,0:T(2,128)(2,1)S(1)}, u32[]{:S(2)}, u32[]{:S(2)}) async-start(bf16[256,2,128]{2,1,0:T(2,128)(2,1)} %add_convert_fusion.1), calls=%async_computation.2 | async-start | bytes 262144 | tf_op jit(solution)/shard_map/all_to_all | solution.py:106
  (203 shorter events, 115.6 us)
Async XLA Ops:
  0.6 7.6 %copy-start.3 = (bf16[256,16,128]{2,1,0:T(8,128)(2,1)S(1)}, bf16[256,16,128]{2,1,0:T(8,128)(2,1)}, u32[]{:S(2)}) copy-start(bf16[256,16,128]{2,1,0:T(8,128)(2,1)} %param.12) | copy-start | bytes 3145732
  2.3 7.9 %all-to-all-start = ((bf16[64,8,128]{2,0,1:T(8,128)(2,1)}), bf16[64,8,128]{2,0,1:T(8,128)(2,1)S(1)}, u32[]{:S(2)}, u32[]{:S(2)}) async-start(bf16[64,8,128]{2,0,1:T(8,128)(2,1)} %copy.54), calls=%async_computation | async-start | bytes 262144 | tf_op jit(solution)/shard_map/all_to_all | solution.py:75
  5.6 3.5 %copy-start.4 = (bf16[64,8,128]{2,1,0:T(8,128)(2,1)S(1)}, bf16[64,8,128]{2,1,0:T(8,128)(2,1)}, u32[]{:S(2)}) copy-start(bf16[64,8,128]{2,1,0:T(8,128)(2,1)} %param.11) | copy-start | bytes 393220
  5.7 4.2 %copy-start.5 = (s32[8]{0:T(128)S(1)}, s32[8]{0:T(128)}, u32[]{:S(2)}) copy-start(s32[8]{0:T(128)} %param.13) | copy-start | bytes 100
  10.2 8.8 %all-to-all-start.1 = ((bf16[64,8,128]{2,0,1:T(8,128)(2,1)}), bf16[64,8,128]{2,0,1:T(8,128)(2,1)S(1)}, u32[]{:S(2)}, u32[]{:S(2)}) async-start(bf16[64,8,128]{2,0,1:T(8,128)(2,1)} %copy.56), calls=%async_computation.1 | async-start | bytes 262144 | tf_op jit(solution)/shard_map/all_to_all | solution.py:76
  13.6 8.2 %collective-permute-start = (bf16[256,2,128]{2,0,1:T(8,128)(2,1)S(1)}, bf16[256,2,128]{2,0,1:T(8,128)(2,1)S(1)}, u32[]{:S(2)}, u32[]{:S(2)}) collective-permute-start(bf16[256,2,128]{2,0,1:T(8,128)(2,1)S(1)} %bitcast.217), channel_id=1, source_target_pairs={{0,4},{4,8},{8,12},{12,16},{16,20},{20,24},{24,28},{1,5},{5,9},{9,... | collective-permute-start | bytes 393224 | tf_op jit(solution)/shard_map/ppermute | solution.py:12
  17.1 11.7 %collective-permute-start.2 = (bf16[256,2,128]{2,0,1:T(8,128)(2,1)S(1)}, bf16[256,2,128]{2,0,1:T(8,128)(2,1)S(1)}, u32[]{:S(2)}, u32[]{:S(2)}) collective-permute-start(bf16[256,2,128]{2,0,1:T(8,128)(2,1)S(1)} %bitcast.218), channel_id=1, source_target_pairs={{0,8},{4,12},{8,16},{12,20},{16,24},{20,28},{1,9},{5,13},{9,17},{1... | collective-permute-start | bytes 393224 | tf_op jit(solution)/shard_map/ppermute | solution.py:12
  19.0 7.8 %collective-permute-start.3 = (bf16[256,2,128]{2,0,1:T(8,128)(2,1)S(1)}, bf16[256,2,128]{2,0,1:T(8,128)(2,1)S(1)}, u32[]{:S(2)}, u32[]{:S(2)}) collective-permute-start(bf16[256,2,128]{2,0,1:T(8,128)(2,1)S(1)} %bitcast.220), channel_id=1, source_target_pairs={{0,4},{4,8},{8,12},{12,16},{16,20},{20,24},{24,28},{1,5},{5,9},{9,... | collective-permute-start | bytes 393224 | tf_op jit(solution)/shard_map/ppermute | solution.py:12
  21.8 9.6 %collective-permute-start.1 = (bf16[256,2,128]{2,0,1:T(8,128)(2,1)S(1)}, bf16[256,2,128]{2,0,1:T(8,128)(2,1)S(1)}, u32[]{:S(2)}, u32[]{:S(2)}) collective-permute-start(bf16[256,2,128]{2,0,1:T(8,128)(2,1)S(1)} %collective-permute-done), channel_id=1, source_target_pairs={{0,8},{4,12},{8,16},{12,20},{16,24},{20,28},{1,9},{5,13},{9,17},{1... | collective-permute-start | bytes 393224 | tf_op jit(solution)/shard_map/ppermute | solution.py:12
  24.9 9.3 %collective-permute-start.5 = (bf16[256,2,128]{2,0,1:T(8,128)(2,1)S(1)}, bf16[256,2,128]{2,0,1:T(8,128)(2,1)S(1)}, u32[]{:S(2)}, u32[]{:S(2)}) collective-permute-start(bf16[256,2,128]{2,0,1:T(8,128)(2,1)S(1)} %bitcast.221), channel_id=1, source_target_pairs={{0,8},{4,12},{8,16},{12,20},{16,24},{20,28},{1,9},{5,13},{9,17},{1... | collective-permute-start | bytes 393224 | tf_op jit(solution)/shard_map/ppermute | solution.py:12
  26.9 9.3 %collective-permute-start.4 = (bf16[256,2,128]{2,0,1:T(8,128)(2,1)S(1)}, bf16[256,2,128]{2,0,1:T(8,128)(2,1)S(1)}, u32[]{:S(2)}, u32[]{:S(2)}) collective-permute-start(bf16[256,2,128]{2,0,1:T(8,128)(2,1)S(1)} %collective-permute-done.3), channel_id=1, source_target_pairs={{0,8},{4,12},{8,16},{12,20},{16,24},{20,28},{1,9},{5,13},{9,17},{1... | collective-permute-start | bytes 393224 | tf_op jit(solution)/shard_map/ppermute | solution.py:12
  89.1 2.3 %copy-start = (bf16[8,256,128]{1,2,0:T(8,128)(2,1)}, bf16[8,256,128]{1,2,0:T(8,128)(2,1)S(1)}, u32[]{:S(2)}) copy-start(bf16[8,256,128]{1,2,0:T(8,128)(2,1)S(1)} %get-tuple-element.114) | copy-start | bytes 1572868
  89.1 4.6 %copy-start.1 = (bf16[8,256,128]{2,1,0:T(8,128)(2,1)}, bf16[8,256,128]{2,1,0:T(8,128)(2,1)S(1)}, u32[]{:S(2)}) copy-start(bf16[8,256,128]{2,1,0:T(8,128)(2,1)S(1)} %get-tuple-element.116) | copy-start | bytes 1572868
  148.2 14.0 %collective-permute-start.10 = (f32[256,2,128]{2,1,0:T(2,128)}, f32[256,2,128]{2,1,0:T(2,128)}, u32[]{:S(2)}, u32[]{:S(2)}) collective-permute-start(f32[256,2,128]{2,1,0:T(2,128)} %get-tuple-element.369), channel_id=1, source_target_pairs={{8,0},{12,4},{16,8},{20,12},{24,16},{28,20},{9,1},{13,5},{17,9},{2... | collective-permute-start | bytes 786440 | tf_op jit(solution)/shard_map/ppermute | solution.py:12
  155.8 15.3 %copy-start.2 = (bf16[8,256,128]{2,1,0:T(8,128)(2,1)S(1)}, bf16[8,256,128]{2,1,0:T(8,128)(2,1)}, u32[]{:S(2)}) copy-start(bf16[8,256,128]{2,1,0:T(8,128)(2,1)} %copy-done.1) | copy-start | bytes 1572868
  156.3 11.1 %collective-permute-start.7 = (f32[256,2,128]{2,1,0:T(2,128)S(1)}, f32[256,2,128]{2,1,0:T(2,128)S(1)}, u32[]{:S(2)}, u32[]{:S(2)}) collective-permute-start(f32[256,2,128]{2,1,0:T(2,128)S(1)} %get-tuple-element.371), channel_id=1, source_target_pairs={{8,0},{12,4},{16,8},{20,12},{24,16},{28,20},{9,1},{13,5},{17,9},{2... | collective-permute-start | bytes 786440 | tf_op jit(solution)/shard_map/ppermute | solution.py:12
  158.3 14.8 %collective-permute-start.9 = (f32[256,2,128]{2,1,0:T(2,128)}, f32[256,2,128]{2,1,0:T(2,128)S(1)}, u32[]{:S(2)}, u32[]{:S(2)}) collective-permute-start(f32[256,2,128]{2,1,0:T(2,128)} %get-tuple-element.368), channel_id=1, source_target_pairs={{8,0},{12,4},{16,8},{20,12},{24,16},{28,20},{9,1},{13,5},{17,9},{2... | collective-permute-start | bytes 786440 | tf_op jit(solution)/shard_map/ppermute | solution.py:12
  160.2 28.4 %collective-permute-start.6 = (f32[256,2,128]{2,1,0:T(2,128)S(1)}, f32[256,2,128]{2,1,0:T(2,128)}, u32[]{:S(2)}, u32[]{:S(2)}) collective-permute-start(f32[256,2,128]{2,1,0:T(2,128)S(1)} %get-tuple-element.370), channel_id=1, source_target_pairs={{8,0},{12,4},{16,8},{20,12},{24,16},{28,20},{9,1},{13,5},{17,9},{2... | collective-permute-start | bytes 786440 | tf_op jit(solution)/shard_map/ppermute | solution.py:12
  163.4 20.9 %collective-permute-start.11 = (f32[256,2,128]{2,1,0:T(2,128)S(1)}, f32[256,2,128]{2,1,0:T(2,128)S(1)}, u32[]{:S(2)}, u32[]{:S(2)}) collective-permute-start(f32[256,2,128]{2,1,0:T(2,128)S(1)} %fusion.61), channel_id=1, source_target_pairs={{4,0},{8,4},{12,8},{16,12},{20,16},{24,20},{28,24},{5,1},{9,5},{13... | collective-permute-start | bytes 786440 | tf_op jit(solution)/shard_map/ppermute | solution.py:12
  168.5 20.1 %collective-permute-start.8 = (f32[256,2,128]{2,1,0:T(2,128)}, f32[256,2,128]{2,1,0:T(2,128)}, u32[]{:S(2)}, u32[]{:S(2)}) collective-permute-start(f32[256,2,128]{2,1,0:T(2,128)} %fusion.59), channel_id=1, source_target_pairs={{4,0},{8,4},{12,8},{16,12},{20,16},{24,20},{28,24},{5,1},{9,5},{13... | collective-permute-start | bytes 786440 | tf_op jit(solution)/shard_map/ppermute | solution.py:12
  185.2 7.9 %all-to-all-start.3 = ((bf16[256,2,128]{2,1,0:T(2,128)(2,1)}), bf16[256,2,128]{2,1,0:T(2,128)(2,1)S(1)}, u32[]{:S(2)}, u32[]{:S(2)}) async-start(bf16[256,2,128]{2,1,0:T(2,128)(2,1)} %add_convert_fusion), calls=%async_computation.3 | async-start | bytes 262144 | tf_op jit(solution)/shard_map/all_to_all | solution.py:109
  193.1 7.9 %all-to-all-start.2 = ((bf16[256,2,128]{2,1,0:T(2,128)(2,1)}), bf16[256,2,128]{2,1,0:T(2,128)(2,1)S(1)}, u32[]{:S(2)}, u32[]{:S(2)}) async-start(bf16[256,2,128]{2,1,0:T(2,128)(2,1)} %add_convert_fusion.1), calls=%async_computation.2 | async-start | bytes 262144 | tf_op jit(solution)/shard_map/all_to_all | solution.py:106
where the time goes:
time: 204 us; the launch traced here: 202 us
  matrix products  89.9 us (44%)
  starting transfers between devices  42 us (21%)
  other arithmetic  24.1 us (12%)
  waiting for transfers between devices  23.9 us (12%)
  local copies, waits for them, and re-layouts  20.3 us (10%)
    dot_general x16, matrix products, head_pass(): jnp.dot(grad_scores.T, query_rows, preferred_element_type=jnp.float32)  32 us
    ppermute x12, starting transfers between devices, shifted(): return lax.ppermute(block, axis, route)  28.7 us
    dot_general x16, matrix products, head_pass(): jnp.dot(query_rows, key_rows.T, preferred_element_type=jnp.float32)  20.7 us
    ppermute x12, waiting for transfers between devices, shifted(): return lax.ppermute(block, axis, route)  20.2 us
    dot_general x16, matrix products, head_pass(): jnp.dot(probs_low.T, grad_rows, preferred_element_type=jnp.float32)  19.9 us
    another operation x8, local copies, waits for them, and re-layouts  9.37 us
    dot_general x16, matrix products, head_pass(): jnp.dot(probs_low, value_rows, preferred_element_type=jnp.float32)  6.28 us
    unnamed x18, local copies, waits for them, and re-layouts  6.18 us
  transfers between devices with their start and end apart: 16, of which 9 were waited for; matrix products, arithmetic and copies ran while one was open for 10% of the time, Pallas kernels for 0%

commit v1 on v0

v1 whole, which is shorter than its diff:
```python
import functools
import math
import jax
import jax.numpy as jnp
from jax import lax
from jax.experimental import pallas as pl
from jax.experimental.pallas import tpu as pltpu
from jax.sharding import PartitionSpec as P

BACK = 3
LANE = 128
F32 = jnp.float32
BF16 = jnp.bfloat16
NEG = -1e30


def _dot(a, b, ca, cb):
    return lax.dot_general(a, b, (((ca,), (cb,)), ((), ())), preferred_element_type=F32)


def attention_kernel(tok, part, per_group, chunk, windows, lengths_ref, shard_ref, q_ref, g_ref, *refs):
    spans, refs = refs[:BACK + 1], refs[BACK + 1:]
    before, refs = refs[:2 * part], refs[2 * part:]
    att_ref, dq_ref = refs[:2]
    d_refs = refs[2:3 + BACK]
    k_sc, v_sc, kt_sc, vt_sc, dk_sc, dv_sc = refs[3 + BACK:]
    block, heads, head = q_ref.shape
    rows = chunk * per_group
    subs = range(block // chunk)
    scale = head ** -0.5
    c2 = scale * math.log2(math.e)
    step = pl.program_id(0)
    base = shard_ref[0] * tok
    span0 = base - BACK * tok
    docs = lengths_ref.shape[0]

    @pl.when(step == 0)
    def _():
        for i, kv in enumerate(reversed(spans)):
            at = pl.ds(i * tok, tok)
            k = kv[0]
            v = kv[1]
            k_sc[at, :] = k
            v_sc[at, :] = v
            kt_sc[:, at] = k.T
            vt_sc[:, at] = v.T
        dk_sc[...] = jnp.zeros_like(dk_sc)
        dv_sc[...] = jnp.zeros_like(dv_sc)

    p0 = base + step * block
    pos = [p0 + s * chunk - span0 + lax.broadcasted_iota(jnp.int32, (1, rows), 1) // per_group for s in subs]

    def add_doc(d, carry):
        begin, first, vecs = carry
        at = begin - span0
        first = jnp.where(begin <= p0, at, first)
        vecs = tuple(jnp.where(at <= pos[s], at, vecs[s]) for s in subs)
        return begin + lengths_ref[d], first, vecs

    none = jnp.zeros((1, rows), jnp.int32)
    _, first, start = lax.fori_loop(0, docs, add_doc, (jnp.int32(0), jnp.int32(0), (none,) * len(subs)))
    top = BACK * tok + (step + 1) * block
    need = top - first

    def mine(ref):
        wide = ref[...].astype(F32)[:, part * per_group:(part + 1) * per_group, :]
        return [wide[s * chunk:(s + 1) * chunk].reshape(rows, head).astype(BF16) for s in subs]

    def body(width):
        low = pl.multiple_of(top - width, LANE)
        wide = [width - (len(subs) - 1 - s) * chunk for s in subs]
        at = [pl.ds(low, w) for w in wide]
        q, go = mine(q_ref), mine(g_ref)
        s = [_dot(k_sc[at[i], :], q[i], 1, 1) for i in subs]
        dp = [_dot(v_sc[at[i], :], go[i], 1, 1) for i in subs]
        masked = []
        for i in subs:
            w = wide[i]
            key = low + lax.broadcasted_iota(jnp.int32, (w, rows), 0)
            x = jnp.where(key >= start[i], s[i], NEG)
            end = jnp.where(key[w - chunk:] <= pos[i], x[w - chunk:], NEG)
            masked.append(jnp.concatenate([x[:w - chunk], end], 0) if w > chunk else end)
        m = [jnp.max(x, axis=0, keepdims=True) * c2 for x in masked]
        e = [jnp.exp2(masked[i] * c2 - m[i]) for i in subs]
        inv = [1.0 / jnp.sum(x, axis=0, keepdims=True) for x in e]
        p = [e[i] * inv[i] for i in subs]
        corr = [jnp.sum(p[i] * dp[i], axis=0, keepdims=True) for i in subs]
        pb = [x.astype(BF16) for x in p]
        ds = [(p[i] * (dp[i] - corr[i])).astype(BF16) for i in subs]
        ot = [_dot(vt_sc[:, pl.ds(low, width)][:, :wide[i]], pb[i], 1, 0).astype(BF16) for i in subs]
        dqt = [(_dot(kt_sc[:, pl.ds(low, width)][:, :wide[i]], ds[i], 1, 0) * scale).astype(BF16) for i in subs]
        for i in subs:
            dv_sc[at[i], :] += _dot(pb[i], go[i], 1, 0)
            dk_sc[at[i], :] += _dot(ds[i], q[i], 1, 0)
        for n, (out, cols) in enumerate(((att_ref, ot), (dq_ref, dqt))):
            for i in subs:
                new = cols[i].T
                if len(out.shape) == 2:
                    out[i * rows:(i + 1) * rows, :] = new
                    continue
                earlier = [before[2 * j + n][i * rows:(i + 1) * rows, :] for j in range(part)]
                both = [x.astype(F32).reshape(chunk, per_group, head) for x in (*earlier, new)]
                both = jnp.concatenate(both, 1) if len(both) > 1 else both[0]
                out[i * chunk:(i + 1) * chunk] = both.astype(BF16)

    for n, width in enumerate(windows):
        cond = need <= width
        if n:
            cond &= need > windows[n - 1]
        pl.when(cond)(functools.partial(body, width))

    @pl.when(step == pl.num_programs(0) - 1)
    def _():
        for i, out in enumerate(reversed(d_refs)):
            at = pl.ds(i * tok, tok)
            out[0] = (dk_sc[at, :] * scale).astype(out.dtype)
            out[1] = dv_sc[at, :].astype(out.dtype)


def attention(queries, grad_out, kvs, lengths, shard, part, parts, before, block=LANE, chunk=32):
    tok, heads, head = queries.shape
    per_group = heads // parts
    span = (BACK + 1) * tok
    most = BACK * tok + block
    windows = tuple(range(LANE, most + 1, LANE))
    rows = block * per_group
    smem = pl.BlockSpec(memory_space=pltpu.SMEM)
    whole = pl.BlockSpec((2, tok, head), lambda i: (0, 0, 0))
    tall = pl.BlockSpec((block, heads, head), lambda i: (i, 0, 0))
    flat = pl.BlockSpec((rows, head), lambda i: (i, 0))
    last = part == parts - 1
    out = jax.ShapeDtypeStruct(queries.shape if last else (tok * per_group, head), BF16)
    share = jax.ShapeDtypeStruct((2, tok, head), BF16)
    own = jax.ShapeDtypeStruct((2, tok, head), F32)
    return pl.pallas_call(
        functools.partial(attention_kernel, tok, part, per_group, chunk, windows),
        grid=(tok // block,),
        out_shape=(out, out, own) + (share,) * BACK,
        in_specs=[smem, smem, tall, tall] + [whole] * (BACK + 1) + [flat] * (2 * part),
        out_specs=(tall if last else flat,) * 2 + (whole,) * (BACK + 1),
        scratch_shapes=[
            pltpu.VMEM((span, head), BF16),
            pltpu.VMEM((span, head), BF16),
            pltpu.VMEM((head, span), BF16),
            pltpu.VMEM((head, span), BF16),
            pltpu.VMEM((span, head), F32),
            pltpu.VMEM((span, head), F32),
        ],
        compiler_params=pltpu.CompilerParams(
            dimension_semantics=("arbitrary",), vmem_limit_bytes=40 * 2**20),
        cost_estimate=pl.CostEstimate(
            flops=12 * tok * per_group * 2 * tok * head, bytes_accessed=4 * tok * heads * head * 2, transcendentals=0),
        name="attention",
    )(lengths, shard, queries, grad_out, *kvs, *before)


def turn(block, distance):
    n = lax.axis_size("ctx")
    return lax.ppermute(block, "ctx", [(i, (i + distance) % n) for i in range(n)])


def swap(block):
    return lax.ppermute(block, "ctx", [(i, i ^ 1) for i in range(lax.axis_size("ctx"))])


def relay(block, distance):
    n = lax.axis_size("ctx")
    return lax.ppermute(block, "ctx", [(i, i + distance) for i in range(0, n, 2) if 0 <= i + distance < n])


def on_device(queries, keys, values, grad_out, lengths):
    n_head = lax.axis_size("head")
    few, kv_heads, head = keys.shape
    parts = kv_heads // n_head
    tok = queries.shape[0]
    shard = lax.axis_index("ctx").astype(jnp.int32)
    odd = shard % 2 == 1
    both = jnp.stack([keys, values]).reshape(2, few, n_head, parts, head).transpose(2, 3, 0, 1, 4)
    both = lax.all_to_all(both, "head", 0, 0, tiled=True)
    own = [both[:, p].transpose(1, 0, 2, 3).reshape(2, tok, head) for p in range(parts)]
    two = [turn(x, 2) for x in own]
    pair = [swap(x) for x in own]
    three = [turn(x, 1) for x in two]
    one = [jnp.where(odd, x, relay(x, 2)) for x in pair]
    before, totals = [], []
    for p in range(parts):
        attended, d_queries, g0, g1, g2, g3 = attention(
            queries, grad_out, (own[p], one[p], two[p], three[p]), lengths, shard.reshape(1), p, parts, before)
        before += [attended, d_queries]
        back3 = turn(g3, -1)
        back1 = relay(g1, -2)
        back2 = turn((g2.astype(F32) + back3.astype(F32)).astype(BF16), -2)
        back_pair = swap(jnp.where(odd, g1, back1))
        totals.append((g0 + back2.astype(F32) + back_pair.astype(F32)).astype(BF16))
    total = jnp.stack(totals).reshape(parts, 2, n_head, few, head).transpose(2, 1, 3, 0, 4)
    total = lax.all_to_all(total, "head", 0, 0, tiled=True)
    done = total.transpose(1, 2, 0, 3, 4).reshape(2, few, kv_heads, head)
    return attended, d_queries, done[0], done[1]


def solution(mesh):
    split = P("ctx", "head", None)
    fine = P(("ctx", "head"), None, None)
    return jax.shard_map(
        on_device,
        mesh=mesh,
        in_specs=(split, fine, fine, split, P()),
        out_specs=(split, split, fine, fine),
        check_vma=False,
    )
```

time: 204 us -> 71.1 us (0.35)
  the two profiles are of different devices: /device:TPU:18 before, /device:TPU:0 now
where the time goes in v1:
time: 71.1 us; the launch traced here: 71 us
  starting transfers between devices  28.6 us (40%)
  blocking collectives  18.6 us (26%)
  waiting for transfers between devices  13.1 us (18%)
  Pallas kernels  6.97 us (10%)
  local copies, waits for them, and re-layouts  2.55 us (4%)
  between operations  0.88 us (1%)
    ppermute x8, starting transfers between devices, turn(): lax.ppermute(block, 'ctx', [(i, (i + distance) % n) for i in range(n)])  16.2 us
    ppermute x8, waiting for transfers between devices, turn(): lax.ppermute(block, 'ctx', [(i, (i + distance) % n) for i in range(n)])  10.5 us
    all_to_all x1, blocking collectives, on_device(): both = lax.all_to_all(both, 'head', 0, 0, tiled=True)  10.2 us
    ppermute x4, starting transfers between devices, relay(): lax.ppermute(block, 'ctx', [(i, i + distance) for i in range(0, n, 2) if...  8.82 us
    all_to_all x1, blocking collectives, on_device(): total = lax.all_to_all(total, 'head', 0, 0, tiled=True)  8.42 us
    pallas_call x2, Pallas kernels, attention(): pl.pallas_call(functools.partial(attention_kernel, tok, part, per_group,...  6.97 us
    ppermute x4, starting transfers between devices, swap(): lax.ppermute(block, 'ctx', [(i, i ^ 1) for i in range(lax.axis_size('ctx'...  3.62 us
    ppermute x4, waiting for transfers between devices, swap(): lax.ppermute(block, 'ctx', [(i, i ^ 1) for i in range(lax.axis_size('ctx'...  2.58 us
  transfers between devices with their start and end apart: 16, of which 4 were waited for; matrix products, arithmetic and copies ran while one was open for 0% of the time, Pallas kernels for 10%

profile of v1, /device:TPU:0, one launch (start us, length us, event | category | flops | bytes accessed | tf_op | source)
XLA Modules:
  0.0 71.0 jit_solution(13185669477381495643)
XLA Ops:
  0.6 1.0 %copy.13 = bf16[64,8,128]{2,0,1:T(8,128)(2,1)S(1)} copy(bf16[64,8,128]{2,1,0:T(8,128)(2,1)} %param.6) | data formatting | bytes 262144 | tf_op args[1]
  1.6 0.0 copy-start.1
  1.7 0.0 copy-start
  1.7 10.2 %all_to_all.10 = bf16[4,2,2,64,128]{4,3,2,1,0:T(8,128)(2,1)S(1)} all-to-all(bf16[4,2,2,64,128]{4,3,2,1,0:T(8,128)(2,1)S(1)} %maximum_bitcast_fusion), channel_id=1, replica_groups=mesh['ctx'=8,'head'=4] {'head'}, dimensions={0} | all-to-all | bytes 524288 | tf_op jit(solution)/shard_map/all_to_all | solution.py:179
  11.9 1.6 %collective-permute-start.4 = (bf16[2,256,128]{2,1,0:T(8,128)(2,1)S(1)}, bf16[2,256,128]{2,1,0:T(8,128)(2,1)S(1)}, u32[]{:S(2)}, u32[]{:S(2)}) collective-permute-start(bf16[2,256,128]{2,1,0:T(8,128)(2,1)S(1)} %bitcast.25), channel_id=1, source_target_pairs={{0,4},{4,0},{8,12},{12,8},{16,20},{20,16},{24,28},{28,24},{1,5},{5... | collective-permute-start | bytes 393224 | tf_op jit(solution)/shard_map/ppermute | solution.py:163
  13.5 1.6 %collective-permute-start.2 = (bf16[2,256,128]{2,1,0:T(8,128)(2,1)S(1)}, bf16[2,256,128]{2,1,0:T(8,128)(2,1)S(1)}, u32[]{:S(2)}, u32[]{:S(2)}) collective-permute-start(bf16[2,256,128]{2,1,0:T(8,128)(2,1)S(1)} %bitcast.22), channel_id=1, source_target_pairs={{0,8},{4,12},{8,16},{12,20},{16,24},{20,28},{24,0},{28,4},{1,9},{5... | collective-permute-start | bytes 393224 | tf_op jit(solution)/shard_map/ppermute | solution.py:159
  15.1 0.5 collective-permute-start
  15.7 1.6 %collective-permute-start.6 = (bf16[2,256,128]{2,1,0:T(8,128)(2,1)S(1)}, bf16[2,256,128]{2,1,0:T(8,128)(2,1)S(1)}, u32[]{:S(2)}, u32[]{:S(2)}) collective-permute-start(bf16[2,256,128]{2,1,0:T(8,128)(2,1)S(1)} %bitcast.26), channel_id=1, source_target_pairs={{0,8},{4,12},{8,16},{12,20},{16,24},{20,28},{24,0},{28,4},{1,9},{5... | collective-permute-start | bytes 393224 | tf_op jit(solution)/shard_map/ppermute | solution.py:159
  17.3 0.0 collective-permute-done.4
  17.3 3.5 %collective-permute-start.5 = (bf16[2,256,128]{2,1,0:T(8,128)(2,1)S(1)}, bf16[2,256,128]{2,1,0:T(8,128)(2,1)S(1)}, u32[]{:S(2)}, u32[]{:S(2)}) collective-permute-start(bf16[2,256,128]{2,1,0:T(8,128)(2,1)S(1)} %collective-permute-done.4), channel_id=1, source_target_pairs={{0,8},{8,16},{16,24},{1,9},{9,17},{17,25},{2,10},{10,18},{18,26},{... | collective-permute-start | bytes 393224 | tf_op jit(solution)/shard_map/ppermute | solution.py:168
  20.8 0.7 collective-permute-done.2.refs_2_
  21.5 0.1 collective-permute-start.3
  21.6 0.0 collective-permute-done
  21.6 2.8 %collective-permute-start.1 = (bf16[2,256,128]{2,1,0:T(8,128)(2,1)S(1)}, bf16[2,256,128]{2,1,0:T(8,128)(2,1)S(1)}, u32[]{:S(2)}, u32[]{:S(2)}) collective-permute-start(bf16[2,256,128]{2,1,0:T(8,128)(2,1)S(1)} %collective-permute-done), channel_id=1, source_target_pairs={{0,8},{8,16},{16,24},{1,9},{9,17},{17,25},{2,10},{10,18},{18,26},{... | collective-permute-start | bytes 393224 | tf_op jit(solution)/shard_map/ppermute | solution.py:168
  24.4 0.2 collective-permute-start.7
  24.7 0.0 copy-start.2
  24.7 7.4 %collective-permute-done.7.refs_3_ = bf16[2,256,128]{2,1,0:T(8,128)(2,1)S(1)} collective-permute-done((bf16[2,256,128]{2,1,0:T(8,128)(2,1)S(1)}, bf16[2,256,128]{2,1,0:T(8,128)(2,1)S(1)}, u32[]{:S(2)}, u32[]{:S(2)}) %collective-permute-start.7) | collective-permute-done | bytes 131104 | tf_op jit(solution)/shard_map/ppermute | solution.py:159
  32.1 2.9 %attention.2 = (bf16[2048,128]{1,0:T(8,128)(2,1)S(1)}, bf16[2048,128]{1,0:T(8,128)(2,1)S(1)}, f32[2,256,128]{2,1,0:T(8,128)S(1)}, bf16[2,256,128]{2,1,0:T(8,128)...) custom-call(s32[8]{0:T(128)S(1)} %copy-done.2, s32[1]{0:T(128)} %bitcast.shard_ref, ...), custom_call_target="tpu_custom_call" | custom-call | flops 1610612736 | bytes 4194304 | tf_op jit(solution)/shard_map/attention/pallas_call | solution.py:135
  35.0 0.3 collective-permute-start.8
  35.3 1.3 %collective-permute-start.10 = (bf16[2,256,128]{2,1,0:T(8,128)(2,1)S(1)}, bf16[2,256,128]{2,1,0:T(8,128)(2,1)S(1)}, u32[]{:S(2)}, u32[]{:S(2)}) collective-permute-start(bf16[2,256,128]{2,1,0:T(8,128)(2,1)S(1)} %get-tuple-element.23), channel_id=1, source_target_pairs={{8,0},{16,8},{24,16},{9,1},{17,9},{25,17},{10,2},{18,10},{26,18},{... | collective-permute-start | bytes 393224 | tf_op jit(solution)/shard_map/ppermute | solution.py:168
  36.6 4.1 %attention.3 = (bf16[256,16,128]{2,1,0:T(8,128)(2,1)}, bf16[256,16,128]{2,1,0:T(8,128)(2,1)}, f32[2,256,128]{2,1,0:T(8,128)S(1)}, bf16[2,256,128]{2,1,0:T(8,128)...) custom-call(s32[8]{0:T(128)S(1)} %copy-done.2, s32[1]{0:T(128)} %bitcast.shard_ref, ...), custom_call_target="tpu_custom_call" | custom-call | flops 1610612736 | bytes 4194304 | tf_op jit(solution)/shard_map/attention/pallas_call | solution.py:135
  40.7 5.3 %collective-permute-start.12 = (bf16[2,256,128]{2,1,0:T(8,128)(2,1)S(1)}, bf16[2,256,128]{2,1,0:T(8,128)(2,1)S(1)}, u32[]{:S(2)}, u32[]{:S(2)}) collective-permute-start(bf16[2,256,128]{2,1,0:T(8,128)(2,1)S(1)} %get-tuple-element.26), channel_id=1, source_target_pairs={{0,28},{4,0},{8,4},{12,8},{16,12},{20,16},{24,20},{28,24},{1,29},{... | collective-permute-start | bytes 393224 | tf_op jit(solution)/shard_map/ppermute | solution.py:159
  46.0 1.3 %collective-permute-start.14 = (bf16[2,256,128]{2,1,0:T(8,128)(2,1)S(1)}, bf16[2,256,128]{2,1,0:T(8,128)(2,1)S(1)}, u32[]{:S(2)}, u32[]{:S(2)}) collective-permute-start(bf16[2,256,128]{2,1,0:T(8,128)(2,1)S(1)} %get-tuple-element.27), channel_id=1, source_target_pairs={{8,0},{16,8},{24,16},{9,1},{17,9},{25,17},{10,2},{18,10},{26,18},{... | collective-permute-start | bytes 393224 | tf_op jit(solution)/shard_map/ppermute | solution.py:168
  47.4 3.6 %collective-permute-start.9 = (bf16[2,256,128]{2,1,0:T(8,128)(2,1)S(1)}, bf16[2,256,128]{2,1,0:T(8,128)(2,1)S(1)}, u32[]{:S(2)}, u32[]{:S(2)}) collective-permute-start(bf16[2,256,128]{2,1,0:T(8,128)(2,1)S(1)} %add_convert_fusion.3), channel_id=1, source_target_pairs={{0,24},{4,28},{8,0},{12,4},{16,8},{20,12},{24,16},{28,20},{1,25},{... | collective-permute-start | bytes 393224 | tf_op jit(solution)/shard_map/ppermute | solution.py:159
  51.0 1.5 %collective-permute-start.11 = (bf16[2,256,128]{2,1,0:T(8,128)(2,1)S(1)}, bf16[2,256,128]{2,1,0:T(8,128)(2,1)S(1)}, u32[]{:S(2)}, u32[]{:S(2)}) collective-permute-start(bf16[2,256,128]{2,1,0:T(8,128)(2,1)S(1)} %broadcast_select_fusion.1), channel_id=1, source_target_pairs={{0,4},{4,0},{8,12},{12,8},{16,20},{20,16},{24,28},{28,24},{1,5},{5... | collective-permute-start | bytes 393224 | tf_op jit(solution)/shard_map/ppermute | solution.py:163
  52.5 3.5 %collective-permute-start.13 = (bf16[2,256,128]{2,1,0:T(8,128)(2,1)S(1)}, bf16[2,256,128]{2,1,0:T(8,128)(2,1)S(1)}, u32[]{:S(2)}, u32[]{:S(2)}) collective-permute-start(bf16[2,256,128]{2,1,0:T(8,128)(2,1)S(1)} %add_convert_fusion.1), channel_id=1, source_target_pairs={{0,24},{4,28},{8,0},{12,4},{16,8},{20,12},{24,16},{28,20},{1,25},{... | collective-permute-start | bytes 393224 | tf_op jit(solution)/shard_map/ppermute | solution.py:159
  56.0 0.1 collective-permute-start.15
  56.2 2.3 %collective-permute-done.13 = bf16[2,256,128]{2,1,0:T(8,128)(2,1)S(1)} collective-permute-done((bf16[2,256,128]{2,1,0:T(8,128)(2,1)S(1)}, bf16[2,256,128]{2,1,0:T(8,128)(2,1)S(1)}, u32[]{:S(2)}, u32[]{:S(2)}) %collective-permute-start.13) | collective-permute-done | bytes 131104 | tf_op jit(solution)/shard_map/ppermute | solution.py:159
  58.5 2.5 %collective-permute-done.15 = bf16[2,256,128]{2,1,0:T(8,128)(2,1)S(1)} collective-permute-done((bf16[2,256,128]{2,1,0:T(8,128)(2,1)S(1)}, bf16[2,256,128]{2,1,0:T(8,128)(2,1)S(1)}, u32[]{:S(2)}, u32[]{:S(2)}) %collective-permute-start.15) | collective-permute-done | bytes 131104 | tf_op jit(solution)/shard_map/ppermute | solution.py:163
  61.1 8.4 %all_to_all.11 = bf16[4,2,64,2,128]{4,2,1,3,0:T(8,128)(2,1)S(1)} all-to-all(bf16[4,2,64,2,128]{4,2,1,3,0:T(8,128)(2,1)S(1)} %copy_bitcast_fusion), channel_id=1, replica_groups=mesh['ctx'=8,'head'=4] {'head'}, dimensions={0} | all-to-all | bytes 524288 | tf_op jit(solution)/shard_map/all_to_all | solution.py:196
  69.6 0.7 %copy.20 = bf16[64,8,128]{2,1,0:T(8,128)(2,1)} copy(bf16[64,8,128]{2,0,1:T(8,128)(2,1)S(1)} %bitcast.32) | data formatting | bytes 262144
  70.3 0.7 %copy.19 = bf16[64,8,128]{2,1,0:T(8,128)(2,1)} copy(bf16[64,8,128]{2,0,1:T(8,128)(2,1)S(1)} %bitcast.31) | data formatting | bytes 262144
  (30 shorter events, 0.4 us)
Async XLA Ops:
  0.6 1.0 %copy-start.3 = (bf16[64,8,128]{2,1,0:T(8,128)(2,1)S(1)}, bf16[64,8,128]{2,1,0:T(8,128)(2,1)}, u32[]{:S(2)}) copy-start(bf16[64,8,128]{2,1,0:T(8,128)(2,1)} %param.7) | copy-start | bytes 393220
  1.6 30.5 %copy-start.1 = (bf16[256,16,128]{2,1,0:T(8,128)(2,1)S(1)}, bf16[256,16,128]{2,1,0:T(8,128)(2,1)}, u32[]{:S(2)}) copy-start(bf16[256,16,128]{2,1,0:T(8,128)(2,1)} %g_ref.3) | copy-start | bytes 3145732
  1.7 30.4 %copy-start = (bf16[256,16,128]{2,1,0:T(8,128)(2,1)S(1)}, bf16[256,16,128]{2,1,0:T(8,128)(2,1)}, u32[]{:S(2)}) copy-start(bf16[256,16,128]{2,1,0:T(8,128)(2,1)} %q_ref.3) | copy-start | bytes 3145732
  11.9 5.4 %collective-permute-start.4 = (bf16[2,256,128]{2,1,0:T(8,128)(2,1)S(1)}, bf16[2,256,128]{2,1,0:T(8,128)(2,1)S(1)}, u32[]{:S(2)}, u32[]{:S(2)}) collective-permute-start(bf16[2,256,128]{2,1,0:T(8,128)(2,1)S(1)} %bitcast.25), channel_id=1, source_target_pairs={{0,4},{4,0},{8,12},{12,8},{16,20},{20,16},{24,28},{28,24},{1,5},{5... | collective-permute-start | bytes 393224 | tf_op jit(solution)/shard_map/ppermute | solution.py:163
  13.5 8.0 %collective-permute-start.2 = (bf16[2,256,128]{2,1,0:T(8,128)(2,1)S(1)}, bf16[2,256,128]{2,1,0:T(8,128)(2,1)S(1)}, u32[]{:S(2)}, u32[]{:S(2)}) collective-permute-start(bf16[2,256,128]{2,1,0:T(8,128)(2,1)S(1)} %bitcast.22), channel_id=1, source_target_pairs={{0,8},{4,12},{8,16},{12,20},{16,24},{20,28},{24,0},{28,4},{1,9},{5... | collective-permute-start | bytes 393224 | tf_op jit(solution)/shard_map/ppermute | solution.py:159
  15.1 6.4 %collective-permute-start = (bf16[2,256,128]{2,1,0:T(8,128)(2,1)S(1)}, bf16[2,256,128]{2,1,0:T(8,128)(2,1)S(1)}, u32[]{:S(2)}, u32[]{:S(2)}) collective-permute-start(bf16[2,256,128]{2,1,0:T(8,128)(2,1)S(1)} %bitcast.23), channel_id=1, source_target_pairs={{0,4},{4,0},{8,12},{12,8},{16,20},{20,16},{24,28},{28,24},{1,5},{5... | collective-permute-start | bytes 393224 | tf_op jit(solution)/shard_map/ppermute | solution.py:163
  15.7 8.7 %collective-permute-start.6 = (bf16[2,256,128]{2,1,0:T(8,128)(2,1)S(1)}, bf16[2,256,128]{2,1,0:T(8,128)(2,1)S(1)}, u32[]{:S(2)}, u32[]{:S(2)}) collective-permute-start(bf16[2,256,128]{2,1,0:T(8,128)(2,1)S(1)} %bitcast.26), channel_id=1, source_target_pairs={{0,8},{4,12},{8,16},{12,20},{16,24},{20,28},{24,0},{28,4},{1,9},{5... | collective-permute-start | bytes 393224 | tf_op jit(solution)/shard_map/ppermute | solution.py:159
  17.3 7.3 %collective-permute-start.5 = (bf16[2,256,128]{2,1,0:T(8,128)(2,1)S(1)}, bf16[2,256,128]{2,1,0:T(8,128)(2,1)S(1)}, u32[]{:S(2)}, u32[]{:S(2)}) collective-permute-start(bf16[2,256,128]{2,1,0:T(8,128)(2,1)S(1)} %collective-permute-done.4), channel_id=1, source_target_pairs={{0,8},{8,16},{16,24},{1,9},{9,17},{17,25},{2,10},{10,18},{18,26},{... | collective-permute-start | bytes 393224 | tf_op jit(solution)/shard_map/ppermute | solution.py:168
  21.5 15.1 %collective-permute-start.3 = (bf16[2,256,128]{2,1,0:T(8,128)(2,1)S(1)}, bf16[2,256,128]{2,1,0:T(8,128)(2,1)S(1)}, u32[]{:S(2)}, u32[]{:S(2)}) collective-permute-start(bf16[2,256,128]{2,1,0:T(8,128)(2,1)S(1)} %collective-permute-done.2.refs_2_), channel_id=1, source_target_pairs={{0,4},{4,8},{8,12},{12,16},{16,20},{20,24},{24,28},{28,0},{1,5},{5... | collective-permute-start | bytes 393224 | tf_op jit(solution)/shard_map/ppermute | solution.py:159
  21.6 15.0 %collective-permute-start.1 = (bf16[2,256,128]{2,1,0:T(8,128)(2,1)S(1)}, bf16[2,256,128]{2,1,0:T(8,128)(2,1)S(1)}, u32[]{:S(2)}, u32[]{:S(2)}) collective-permute-start(bf16[2,256,128]{2,1,0:T(8,128)(2,1)S(1)} %collective-permute-done), channel_id=1, source_target_pairs={{0,8},{8,16},{16,24},{1,9},{9,17},{17,25},{2,10},{10,18},{18,26},{... | collective-permute-start | bytes 393224 | tf_op jit(solution)/shard_map/ppermute | solution.py:168
  24.4 7.7 %collective-permute-start.7 = (bf16[2,256,128]{2,1,0:T(8,128)(2,1)S(1)}, bf16[2,256,128]{2,1,0:T(8,128)(2,1)S(1)}, u32[]{:S(2)}, u32[]{:S(2)}) collective-permute-start(bf16[2,256,128]{2,1,0:T(8,128)(2,1)S(1)} %collective-permute-done.6.refs_2_), channel_id=1, source_target_pairs={{0,4},{4,8},{8,12},{12,16},{16,20},{20,24},{24,28},{28,0},{1,5},{5... | collective-permute-start | bytes 393224 | tf_op jit(solution)/shard_map/ppermute | solution.py:159
  24.7 7.5 %copy-start.2 = (s32[8]{0:T(128)S(1)}, s32[8]{0:T(128)}, u32[]{:S(2)}) copy-start(s32[8]{0:T(128)} %lengths_ref.3) | copy-start | bytes 100
  35.0 12.3 %collective-permute-start.8 = (bf16[2,256,128]{2,1,0:T(8,128)(2,1)S(1)}, bf16[2,256,128]{2,1,0:T(8,128)(2,1)S(1)}, u32[]{:S(2)}, u32[]{:S(2)}) collective-permute-start(bf16[2,256,128]{2,1,0:T(8,128)(2,1)S(1)} %get-tuple-element.22), channel_id=1, source_target_pairs={{0,28},{4,0},{8,4},{12,8},{16,12},{20,16},{24,20},{28,24},{1,29},{... | collective-permute-start | bytes 393224 | tf_op jit(solution)/shard_map/ppermute | solution.py:159
  35.3 15.7 %collective-permute-start.10 = (bf16[2,256,128]{2,1,0:T(8,128)(2,1)S(1)}, bf16[2,256,128]{2,1,0:T(8,128)(2,1)S(1)}, u32[]{:S(2)}, u32[]{:S(2)}) collective-permute-start(bf16[2,256,128]{2,1,0:T(8,128)(2,1)S(1)} %get-tuple-element.23), channel_id=1, source_target_pairs={{8,0},{16,8},{24,16},{9,1},{17,9},{25,17},{10,2},{18,10},{26,18},{... | collective-permute-start | bytes 393224 | tf_op jit(solution)/shard_map/ppermute | solution.py:168
  40.7 11.7 %collective-permute-start.12 = (bf16[2,256,128]{2,1,0:T(8,128)(2,1)S(1)}, bf16[2,256,128]{2,1,0:T(8,128)(2,1)S(1)}, u32[]{:S(2)}, u32[]{:S(2)}) collective-permute-start(bf16[2,256,128]{2,1,0:T(8,128)(2,1)S(1)} %get-tuple-element.26), channel_id=1, source_target_pairs={{0,28},{4,0},{8,4},{12,8},{16,12},{20,16},{24,20},{28,24},{1,29},{... | collective-permute-start | bytes 393224 | tf_op jit(solution)/shard_map/ppermute | solution.py:159
  46.0 10.0 %collective-permute-start.14 = (bf16[2,256,128]{2,1,0:T(8,128)(2,1)S(1)}, bf16[2,256,128]{2,1,0:T(8,128)(2,1)S(1)}, u32[]{:S(2)}, u32[]{:S(2)}) collective-permute-start(bf16[2,256,128]{2,1,0:T(8,128)(2,1)S(1)} %get-tuple-element.27), channel_id=1, source_target_pairs={{8,0},{16,8},{24,16},{9,1},{17,9},{25,17},{10,2},{18,10},{26,18},{... | collective-permute-start | bytes 393224 | tf_op jit(solution)/shard_map/ppermute | solution.py:168
  47.4 8.7 %collective-permute-start.9 = (bf16[2,256,128]{2,1,0:T(8,128)(2,1)S(1)}, bf16[2,256,128]{2,1,0:T(8,128)(2,1)S(1)}, u32[]{:S(2)}, u32[]{:S(2)}) collective-permute-start(bf16[2,256,128]{2,1,0:T(8,128)(2,1)S(1)} %add_convert_fusion.3), channel_id=1, source_target_pairs={{0,24},{4,28},{8,0},{12,4},{16,8},{20,12},{24,16},{28,20},{1,25},{... | collective-permute-start | bytes 393224 | tf_op jit(solution)/shard_map/ppermute | solution.py:159
  51.0 5.1 %collective-permute-start.11 = (bf16[2,256,128]{2,1,0:T(8,128)(2,1)S(1)}, bf16[2,256,128]{2,1,0:T(8,128)(2,1)S(1)}, u32[]{:S(2)}, u32[]{:S(2)}) collective-permute-start(bf16[2,256,128]{2,1,0:T(8,128)(2,1)S(1)} %broadcast_select_fusion.1), channel_id=1, source_target_pairs={{0,4},{4,0},{8,12},{12,8},{16,20},{20,16},{24,28},{28,24},{1,5},{5... | collective-permute-start | bytes 393224 | tf_op jit(solution)/shard_map/ppermute | solution.py:163
  52.5 6.0 %collective-permute-start.13 = (bf16[2,256,128]{2,1,0:T(8,128)(2,1)S(1)}, bf16[2,256,128]{2,1,0:T(8,128)(2,1)S(1)}, u32[]{:S(2)}, u32[]{:S(2)}) collective-permute-start(bf16[2,256,128]{2,1,0:T(8,128)(2,1)S(1)} %add_convert_fusion.1), channel_id=1, source_target_pairs={{0,24},{4,28},{8,0},{12,4},{16,8},{20,12},{24,16},{28,20},{1,25},{... | collective-permute-start | bytes 393224 | tf_op jit(solution)/shard_map/ppermute | solution.py:159
  56.0 5.0 %collective-permute-start.15 = (bf16[2,256,128]{2,1,0:T(8,128)(2,1)S(1)}, bf16[2,256,128]{2,1,0:T(8,128)(2,1)S(1)}, u32[]{:S(2)}, u32[]{:S(2)}) collective-permute-start(bf16[2,256,128]{2,1,0:T(8,128)(2,1)S(1)} %broadcast_select_fusion), channel_id=1, source_target_pairs={{0,4},{4,0},{8,12},{12,8},{16,20},{20,16},{24,28},{28,24},{1,5},{5... | collective-permute-start | bytes 393224 | tf_op jit(solution)/shard_map/ppermute | solution.py:163

commit v2 on v1

v2 whole, which is shorter than its diff:
```python
import functools
import math
import jax
import jax.numpy as jnp
from jax import lax
from jax.experimental import pallas as pl
from jax.experimental.pallas import tpu as pltpu
from jax.sharding import PartitionSpec as P

BACK = 3
LANE = 128
F32 = jnp.float32
BF16 = jnp.bfloat16
NEG = -1e30


def _dot(a, b, ca, cb):
    return lax.dot_general(a, b, (((ca,), (cb,)), ((), ())), preferred_element_type=F32)


def attention_kernel(tok, few, chunk, windows, lengths_ref, place_ref, q_ref, g_ref, *refs):
    spans, refs = refs[:BACK + 1], refs[BACK + 1:]
    (att_ref, dq_ref), d_refs = refs[:2], refs[2:3 + BACK]
    k_sc, v_sc, kt_sc, vt_sc, dk_sc, dv_sc = refs[3 + BACK:]
    block, heads, head = q_ref.shape
    groups = k_sc.shape[0]
    per_group = heads // groups
    rows = chunk * per_group
    subs = range(block // chunk)
    scale = head ** -0.5
    c2 = scale * math.log2(math.e)
    step = pl.program_id(0)
    base = place_ref[0] * tok
    span0 = base - BACK * tok
    docs = lengths_ref.shape[0]

    def place(i, s):
        return pl.ds(pl.multiple_of(i * tok + (place_ref[1] ^ s) * few, few), few)

    @pl.when(step == 0)
    def _():
        for i, kv in enumerate(reversed(spans)):
            for g in range(groups):
                lanes = slice(g * head, (g + 1) * head)
                for s in range(tok // few):
                    part = slice(s * few, (s + 1) * few)
                    k_sc[g, place(i, s), :] = kv[0, part, lanes]
                    v_sc[g, place(i, s), :] = kv[1, part, lanes]
                at = pl.ds(i * tok, tok)
                kt_sc[g, :, at] = k_sc[g, at, :].T
                vt_sc[g, :, at] = v_sc[g, at, :].T
        dk_sc[...] = jnp.zeros_like(dk_sc)
        dv_sc[...] = jnp.zeros_like(dv_sc)

    p0 = base + step * block
    pos = [p0 + s * chunk - span0 + lax.broadcasted_iota(jnp.int32, (1, rows), 1) // per_group for s in subs]

    def add_doc(d, carry):
        begin, first, vecs = carry
        at = begin - span0
        first = jnp.where(begin <= p0, at, first)
        vecs = tuple(jnp.where(at <= pos[s], at, vecs[s]) for s in subs)
        return begin + lengths_ref[d], first, vecs

    none = jnp.zeros((1, rows), jnp.int32)
    _, first, start = lax.fori_loop(0, docs, add_doc, (jnp.int32(0), jnp.int32(0), (none,) * len(subs)))
    top = BACK * tok + (step + 1) * block
    need = top - first

    def mine(ref, g):
        wide = ref[...].astype(F32)[:, g * per_group:(g + 1) * per_group, :]
        return [wide[s * chunk:(s + 1) * chunk].reshape(rows, head).astype(BF16) for s in subs]

    def one_group(g, low, width):
        wide = [width - (len(subs) - 1 - s) * chunk for s in subs]
        at = [pl.ds(low, w) for w in wide]
        q, go = mine(q_ref, g), mine(g_ref, g)
        s = [_dot(k_sc[g, at[i], :], q[i], 1, 1) for i in subs]
        dp = [_dot(v_sc[g, at[i], :], go[i], 1, 1) for i in subs]
        masked = []
        for i in subs:
            w = wide[i]
            key = low + lax.broadcasted_iota(jnp.int32, (w, rows), 0)
            x = jnp.where(key >= start[i], s[i], NEG)
            end = jnp.where(key[w - chunk:] <= pos[i], x[w - chunk:], NEG)
            masked.append(jnp.concatenate([x[:w - chunk], end], 0) if w > chunk else end)
        m = [jnp.max(x, axis=0, keepdims=True) * c2 for x in masked]
        e = [jnp.exp2(masked[i] * c2 - m[i]) for i in subs]
        inv = [1.0 / jnp.sum(x, axis=0, keepdims=True) for x in e]
        p = [e[i] * inv[i] for i in subs]
        corr = [jnp.sum(p[i] * dp[i], axis=0, keepdims=True) for i in subs]
        pb = [x.astype(BF16) for x in p]
        ds = [(p[i] * (dp[i] - corr[i])).astype(BF16) for i in subs]
        ot = [_dot(vt_sc[g, :, pl.ds(low, width)][:, :wide[i]], pb[i], 1, 0).astype(BF16) for i in subs]
        dqt = [(_dot(kt_sc[g, :, pl.ds(low, width)][:, :wide[i]], ds[i], 1, 0) * scale).astype(BF16) for i in subs]
        for i in subs:
            dv_sc[g, at[i], :] += _dot(pb[i], go[i], 1, 0)
            dk_sc[g, at[i], :] += _dot(ds[i], q[i], 1, 0)
        return [[x.T.astype(F32).reshape(chunk, per_group, head) for x in y] for y in (ot, dqt)]

    def body(width):
        low = pl.multiple_of(top - width, LANE)
        done = [one_group(g, low, width) for g in range(groups)]
        for n, out in enumerate((att_ref, dq_ref)):
            for i in subs:
                both = [done[g][n][i] for g in range(groups)]
                both = jnp.concatenate(both, 1) if groups > 1 else both[0]
                out[i * chunk:(i + 1) * chunk] = both.astype(BF16)

    for n, width in enumerate(windows):
        cond = need <= width
        if n:
            cond &= need > windows[n - 1]
        pl.when(cond)(functools.partial(body, width))

    @pl.when(step == pl.num_programs(0) - 1)
    def _():
        for i, out in enumerate(reversed(d_refs)):
            for g in range(groups):
                lanes = slice(g * head, (g + 1) * head)
                for s in range(tok // few):
                    part = slice(s * few, (s + 1) * few)
                    out[0, part, lanes] = (dk_sc[g, place(i, s), :] * scale).astype(out.dtype)
                    out[1, part, lanes] = dv_sc[g, place(i, s), :].astype(out.dtype)


def attention(queries, grad_out, kvs, lengths, place, few, block=LANE, chunk=32):
    tok, heads, head = queries.shape
    lanes = kvs[0].shape[2]
    groups = lanes // head
    span = (BACK + 1) * tok
    most = BACK * tok + block
    windows = tuple(range(LANE, most + 1, LANE))
    smem = pl.BlockSpec(memory_space=pltpu.SMEM)
    whole = pl.BlockSpec((2, tok, lanes), lambda i: (0, 0, 0))
    tall = pl.BlockSpec((block, heads, head), lambda i: (i, 0, 0))
    out = jax.ShapeDtypeStruct(queries.shape, BF16)
    share = jax.ShapeDtypeStruct((2, tok, lanes), BF16)
    own = jax.ShapeDtypeStruct((2, tok, lanes), F32)
    return pl.pallas_call(
        functools.partial(attention_kernel, tok, few, chunk, windows),
        grid=(tok // block,),
        out_shape=(out, out, own) + (share,) * BACK,
        in_specs=[smem, smem, tall, tall] + [whole] * (BACK + 1),
        out_specs=(tall, tall) + (whole,) * (BACK + 1),
        scratch_shapes=[
            pltpu.VMEM((groups, span, head), BF16),
            pltpu.VMEM((groups, span, head), BF16),
            pltpu.VMEM((groups, head, span), BF16),
            pltpu.VMEM((groups, head, span), BF16),
            pltpu.VMEM((groups, span, head), F32),
            pltpu.VMEM((groups, span, head), F32),
        ],
        compiler_params=pltpu.CompilerParams(
            dimension_semantics=("arbitrary",), vmem_limit_bytes=40 * 2**20),
        cost_estimate=pl.CostEstimate(
            flops=12 * tok * heads * 2 * tok * head, bytes_accessed=4 * tok * heads * head * 2, transcendentals=0),
        name="attention",
    )(lengths, place, queries, grad_out, *kvs)


def route(block, distance, flip):
    n, m = lax.axis_size("ctx"), lax.axis_size("head")
    if distance == 0:
        return lax.ppermute(block, "head", [(h, h ^ flip) for h in range(m)])
    to = [c ^ 1 if distance is None else (c + distance) % n for c in range(n)]
    if flip == 0:
        return lax.ppermute(block, "ctx", [(c, to[c]) for c in range(n)])
    return lax.ppermute(block, ("ctx", "head"), [(c * m + h, to[c] * m + (h ^ flip)) for c in range(n) for h in range(m)])


def relay(block, distance):
    n = lax.axis_size("ctx")
    return lax.ppermute(block, "ctx", [(i, i + distance) for i in range(0, n, 2) if 0 <= i + distance < n])


def reorder(pieces, me):
    n, bit = len(pieces), 1
    while bit < n:
        on = (me & bit) != 0
        pieces = [jnp.where(on, pieces[i ^ bit], pieces[i]) for i in range(n)]
        bit *= 2
    return pieces


def gather(keys, values, me, odd):
    n = lax.axis_size("head")
    few, kv_heads, head = keys.shape
    lanes = kv_heads // n * head
    both = jnp.stack([keys, values]).reshape(2, few, n, lanes)
    pieces = reorder([both[:, :, i] for i in range(n)], me)
    got = route(jnp.stack(pieces[1::2]), 0, 1)
    mine = [jnp.concatenate([pieces[2 * u], got[u]], 1) for u in range(n // 2)]
    def assembled(distance):
        return jnp.concatenate([x if distance == 0 and u == 0 else route(x, distance, 2 * u) for u, x in enumerate(mine)], 1)
    two, pair, own = assembled(2), assembled(None), assembled(0)
    three = route(two, 1, 0)
    one = jnp.where(odd, pair, relay(pair, 2))
    return own, one, two, three

def scatter(own, one, two, three, me, odd):
    n = lax.axis_size("head")
    few = own.shape[1] // n
    near = route(one, None, 0).astype(F32)
    far = route(three, -1, 0).astype(F32)
    two = (two.astype(F32) + far + jnp.where(odd, near, 0.0)).astype(BF16)
    own = own + jnp.where(odd, 0.0, near)
    sums = []
    for u in range(n // 2):
        at = slice(2 * u * few, 2 * (u + 1) * few)
        base = own[:, at] if u == 0 else route(own[:, at].astype(BF16), 0, 2 * u).astype(F32)
        sums.append((base + route(two[:, at], -2, 2 * u).astype(F32)).astype(BF16))
    got = route(jnp.stack([x[:, few:] for x in sums]), 0, 1)
    pieces = [x for u in range(n // 2) for x in (sums[u][:, :few], got[u])]
    return jnp.stack(reorder(pieces, me), 2)


def on_device(queries, keys, values, grad_out, lengths):
    shard = lax.axis_index("ctx").astype(jnp.int32)
    me = lax.axis_index("head").astype(jnp.int32)
    odd = shard % 2 == 1
    spans = gather(keys, values, me, odd)
    attended, d_queries, *grads = attention(
        queries, grad_out, spans, lengths, jnp.stack([shard, me]), keys.shape[0])
    d_keys, d_values = scatter(*grads, me, odd).reshape(2, *keys.shape)
    return attended, d_queries, d_keys, d_values


def solution(mesh):
    split = P("ctx", "head", None)
    fine = P(("ctx", "head"), None, None)
    return jax.shard_map(
        on_device,
        mesh=mesh,
        in_specs=(split, fine, fine, split, P()),
        out_specs=(split, split, fine, fine),
        check_vma=False,
    )
```

time: 71.1 us -> 65.4 us (0.920); the launches traced: 71 us -> 64.6 us
  blocking collectives: 18.6 us -> 0 us
  waiting for transfers between devices: 13.1 us -> 22.6 us
  starting transfers between devices: 28.6 us -> 31.3 us
  Pallas kernels: 6.97 us -> 5.59 us
  local copies, waits for them, and re-layouts: 2.55 us -> 3.76 us
    all_to_all x2 -> x0, blocking collectives: 18.6 us -> none  [the longest x1 10.2 us: on_device(): both = lax.all_to_all(both, 'head', 0, 0, tiled=True)]
    ppermute x12 -> x13, starting transfers between devices: 19.8 us -> 26.5 us  [the longest x6 19.7 us: route(): return lax.ppermute(block, 'ctx', [(c, to[c]) for c in range(n)])]
    ppermute x12 -> x13, waiting for transfers between devices: 13.1 us -> 19.3 us  [the longest x6 10.1 us: route(): return lax.ppermute(block, 'ctx', [(c, to[c]) for c in range(n)])]
    ppermute x4 -> x1, starting transfers between devices: 8.82 us -> 4.88 us  [relay(): lax.ppermute(block, 'ctx', [(i, i + distance) for i in range(0, n, 2) if...]
    ppermute x4 -> x1, waiting for transfers between devices: 0.01 us -> 3.22 us  [relay(): lax.ppermute(block, 'ctx', [(i, i + distance) for i in range(0, n, 2) if...]
    another operation x0 -> x10, local copies, waits for them, and re-layouts: none -> 2.77 us  [the longest x5 1.65 us: on_device(): d_keys, d_values = scatter(*grads, me, odd).reshape(2, *keys.shape)]
    unnamed x12 -> x11, local copies, waits for them, and re-layouts: 2.49 us -> 0.93 us
    pallas_call x2 -> x1, Pallas kernels: 6.97 us -> 5.59 us  [attention(): pl.pallas_call(functools.partial(attention_kernel, tok, few, chunk, windo...]
  transfers between devices with their start and end apart: 16 -> 14, of which waited for: 4 -> 10; matrix products, arithmetic and copies ran while one was open for 0% -> 0% of each run, Pallas kernels for 10% -> 0%
where the time goes in v2:
time: 65.4 us; the launch traced here: 64.6 us
  starting transfers between devices  31.3 us (48%)
  waiting for transfers between devices  22.6 us (35%)
  Pallas kernels  5.59 us (9%)
  local copies, waits for them, and re-layouts  3.76 us (6%)
  between operations  0.87 us (1%)
    ppermute x6, starting transfers between devices, route(): return lax.ppermute(block, 'ctx', [(c, to[c]) for c in range(n)])  19.7 us
    ppermute x6, waiting for transfers between devices, route(): return lax.ppermute(block, 'ctx', [(c, to[c]) for c in range(n)])  10.1 us
    pallas_call x1, Pallas kernels, attention(): pl.pallas_call(functools.partial(attention_kernel, tok, few, chunk, windo...  5.59 us
    ppermute x4, waiting for transfers between devices, route(): return lax.ppermute(block, 'head', [(h, h ^ flip) for h in range(m)])  5.29 us
    ppermute x1, starting transfers between devices, relay(): lax.ppermute(block, 'ctx', [(i, i + distance) for i in range(0, n, 2) if...  4.88 us
    ppermute x3, waiting for transfers between devices, route(): lax.ppermute(block, ('ctx', 'head'), [(c * m + h, to[c] * m + (h ^ flip))...  3.91 us
    ppermute x4, starting transfers between devices, route(): return lax.ppermute(block, 'head', [(h, h ^ flip) for h in range(m)])  3.57 us
    ppermute x1, waiting for transfers between devices, relay(): lax.ppermute(block, 'ctx', [(i, i + distance) for i in range(0, n, 2) if...  3.22 us
  transfers between devices with their start and end apart: 14, of which 10 were waited for; matrix products, arithmetic and copies ran while one was open for 0% of the time, Pallas kernels for 0%

profile of v2, /device:TPU:0, one launch (start us, length us, event | category | flops | bytes accessed | tf_op | source)
XLA Modules:
  0.0 64.6 jit_solution(2550864950920520443)
XLA Ops:
  0.6 1.0 %stack.50 = bf16[1,64,4,256]{3,2,1,0:T(4,128)(2,1)S(1)} reshape(bf16[64,8,128]{2,1,0:T(8,128)(2,1)} %param.6) | data formatting | bytes 262144 | tf_op jit(solution)/shard_map/stack | solution.py:190
  1.7 0.9 %copy-done.3 = bf16[64,8,128]{2,1,0:T(8,128)(2,1)S(1)} copy-done((bf16[64,8,128]{2,1,0:T(8,128)(2,1)S(1)}, bf16[64,8,128]{2,1,0:T(8,128)(2,1)}, u32[]{:S(2)}) %copy-start.3) | copy-done | bytes 131096
  2.5 0.1 stack.51
  2.7 0.5 collective-permute-start
  3.2 1.0 %collective-permute-done = bf16[2,2,64,256]{3,2,1,0:T(8,128)(2,1)S(1)} collective-permute-done((bf16[2,2,64,256]{3,2,1,0:T(8,128)(2,1)S(1)}, bf16[2,2,64,256]{3,2,1,0:T(8,128)(2,1)S(1)}, u32[]{:S(2)}, u32[]{:S(2)}) %collective-permute-start) | collective-permute-done | bytes 131104 | tf_op jit(solution)/shard_map/ppermute | solution.py:165
  4.3 2.9 %collective-permute-start.2 = (bf16[2,128,256]{2,1,0:T(8,128)(2,1)S(1)}, bf16[2,128,256]{2,1,0:T(8,128)(2,1)S(1)}, u32[]{:S(2)}, u32[]{:S(2)}) collective-permute-start(bf16[2,128,256]{2,1,0:T(8,128)(2,1)S(1)} %pad_maximum_fusion.4), channel_id=1, source_target_pairs={{0,4},{4,0},{8,12},{12,8},{16,20},{20,16},{24,28},{28,24},{1,5},{5... | collective-permute-start | bytes 393224 | tf_op jit(solution)/shard_map/ppermute | solution.py:168
  7.2 1.6 %collective-permute-start.3 = (bf16[2,128,256]{2,1,0:T(8,128)(2,1)S(1)}, bf16[2,128,256]{2,1,0:T(8,128)(2,1)S(1)}, u32[]{:S(2)}, u32[]{:S(2)}) collective-permute-start(bf16[2,128,256]{2,1,0:T(8,128)(2,1)S(1)} %pad_maximum_fusion.3), channel_id=1, source_target_pairs={{0,6},{1,7},{2,4},{3,5},{4,2},{5,3},{6,0},{7,1},{8,14},{9,15},{10,... | collective-permute-start | bytes 393224 | tf_op jit(solution)/shard_map/ppermute | solution.py:169
  8.7 0.1 pad_add_fusion.place_ref
  8.8 1.6 %collective-permute-start.5 = (bf16[2,128,256]{2,1,0:T(8,128)(2,1)S(1)}, bf16[2,128,256]{2,1,0:T(8,128)(2,1)S(1)}, u32[]{:S(2)}, u32[]{:S(2)}) collective-permute-start(bf16[2,128,256]{2,1,0:T(8,128)(2,1)S(1)} %pad_maximum_fusion.4), channel_id=1, source_target_pairs={{0,8},{4,12},{8,16},{12,20},{16,24},{20,28},{24,0},{28,4},{1,9},{5... | collective-permute-start | bytes 393224 | tf_op jit(solution)/shard_map/ppermute | solution.py:168
  10.4 1.5 %collective-permute-start.6 = (bf16[2,128,256]{2,1,0:T(8,128)(2,1)S(1)}, bf16[2,128,256]{2,1,0:T(8,128)(2,1)S(1)}, u32[]{:S(2)}, u32[]{:S(2)}) collective-permute-start(bf16[2,128,256]{2,1,0:T(8,128)(2,1)S(1)} %pad_maximum_fusion.3), channel_id=1, source_target_pairs={{0,10},{1,11},{2,8},{3,9},{4,14},{5,15},{6,12},{7,13},{8,18},{9,19... | collective-permute-start | bytes 393224 | tf_op jit(solution)/shard_map/ppermute | solution.py:169
  11.9 1.5 %collective-permute-start.1 = (bf16[2,128,256]{2,1,0:T(8,128)(2,1)S(1)}, bf16[2,128,256]{2,1,0:T(8,128)(2,1)S(1)}, u32[]{:S(2)}, u32[]{:S(2)}) collective-permute-start(bf16[2,128,256]{2,1,0:T(8,128)(2,1)S(1)} %pad_maximum_fusion.3), channel_id=1, source_target_pairs={{0,2},{1,3},{2,0},{3,1},{4,6},{5,7},{6,4},{7,5},{8,10},{9,11},{10,... | collective-permute-start | bytes 393224 | tf_op jit(solution)/shard_map/ppermute | solution.py:165
  13.5 1.6 %collective-permute-done.3 = bf16[2,128,256]{2,1,0:T(8,128)(2,1)S(1)} collective-permute-done((bf16[2,128,256]{2,1,0:T(8,128)(2,1)S(1)}, bf16[2,128,256]{2,1,0:T(8,128)(2,1)S(1)}, u32[]{:S(2)}, u32[]{:S(2)}) %collective-permute-start.3) | collective-permute-done | bytes 131104 | tf_op jit(solution)/shard_map/ppermute | solution.py:169
  15.1 4.9 %collective-permute-start.4 = (bf16[2,256,256]{2,1,0:T(8,128)(2,1)S(1)}, bf16[2,256,256]{2,1,0:T(8,128)(2,1)S(1)}, u32[]{:S(2)}, u32[]{:S(2)}) collective-permute-start(bf16[2,256,256]{2,1,0:T(8,128)(2,1)S(1)} %constant_dynamic-update-slice_fusion), channel_id=1, source_target_pairs={{0,8},{8,16},{16,24},{1,9},{9,17},{17,25},{2,10},{10,18},{18,26},{... | collective-permute-start | bytes 786440 | tf_op jit(solution)/shard_map/ppermute | solution.py:174
  20.1 0.5 collective-permute-done.1
  20.6 3.2 %collective-permute-done.4 = bf16[2,256,256]{2,1,0:T(8,128)(2,1)S(1)} collective-permute-done((bf16[2,256,256]{2,1,0:T(8,128)(2,1)S(1)}, bf16[2,256,256]{2,1,0:T(8,128)(2,1)S(1)}, u32[]{:S(2)}, u32[]{:S(2)}) %collective-permute-start.4) | collective-permute-done | bytes 262176 | tf_op jit(solution)/shard_map/ppermute | solution.py:174
  23.9 5.3 %collective-permute-done.7.refs_3_ = bf16[2,256,256]{2,1,0:T(8,128)(2,1)S(1)} collective-permute-done((bf16[2,256,256]{2,1,0:T(8,128)(2,1)S(1)}, bf16[2,256,256]{2,1,0:T(8,128)(2,1)S(1)}, u32[]{:S(2)}, u32[]{:S(2)}) %collective-permute-start.7) | collective-permute-done | bytes 262176 | tf_op jit(solution)/shard_map/ppermute | solution.py:168
  29.2 5.6 %attention.1 = (bf16[256,16,128]{2,1,0:T(8,128)(2,1)}, bf16[256,16,128]{2,1,0:T(8,128)(2,1)}, f32[2,256,256]{2,1,0:T(8,128)S(1)}, bf16[2,256,256]{2,1,0:T(8,128)...) custom-call(s32[8]{0:T(128)S(1)} %copy-done.2, s32[2]{0:T(128)S(1)} %pad_add_fusion.place_ref, ...), custom_call_target="tpu_custom_call" | custom-call | flops 3221225472 | bytes 4194304 | tf_op jit(solution)/shard_map/attention/pallas_call | solution.py:140
  34.8 9.4 %collective-permute-start.9 = (bf16[2,256,256]{2,1,0:T(8,128)(2,1)S(1)}, bf16[2,256,256]{2,1,0:T(8,128)(2,1)S(1)}, u32[]{:S(2)}, u32[]{:S(2)}) collective-permute-start(bf16[2,256,256]{2,1,0:T(8,128)(2,1)S(1)} %get-tuple-element.15), channel_id=1, source_target_pairs={{0,28},{4,0},{8,4},{12,8},{16,12},{20,16},{24,20},{28,24},{1,29},{... | collective-permute-start | bytes 786440 | tf_op jit(solution)/shard_map/ppermute | solution.py:168
  44.1 3.9 %collective-permute-done.9 = bf16[2,256,256]{2,1,0:T(8,128)(2,1)S(1)} collective-permute-done((bf16[2,256,256]{2,1,0:T(8,128)(2,1)S(1)}, bf16[2,256,256]{2,1,0:T(8,128)(2,1)S(1)}, u32[]{:S(2)}, u32[]{:S(2)}) %collective-permute-start.9) | collective-permute-done | bytes 262176 | tf_op jit(solution)/shard_map/ppermute | solution.py:168
  48.0 0.2 fusion
  48.2 5.8 %collective-permute-start.10 = (bf16[2,128,256]{2,1,0:T(8,128)(2,1)S(1)}, bf16[2,128,256]{2,1,0:T(8,128)(2,1)S(1)}, u32[]{:S(2)}, u32[]{:S(2)}) collective-permute-start(bf16[2,128,256]{2,1,0:T(8,128)(2,1)S(1)} %get-tuple-element.22), channel_id=1, source_target_pairs={{0,24},{4,28},{8,0},{12,4},{16,8},{20,12},{24,16},{28,20},{1,25},{... | collective-permute-start | bytes 393224 | tf_op jit(solution)/shard_map/ppermute | solution.py:168
  54.1 1.5 %collective-permute-start.11 = (bf16[2,128,256]{2,1,0:T(8,128)(2,1)S(1)}, bf16[2,128,256]{2,1,0:T(8,128)(2,1)S(1)}, u32[]{:S(2)}, u32[]{:S(2)}) collective-permute-start(bf16[2,128,256]{2,1,0:T(8,128)(2,1)S(1)} %slice.177), channel_id=1, source_target_pairs={{0,2},{1,3},{2,0},{3,1},{4,6},{5,7},{6,4},{7,5},{8,10},{9,11},{10,... | collective-permute-start | bytes 393224 | tf_op jit(solution)/shard_map/ppermute | solution.py:165
  55.5 0.1 collective-permute-start.12
  55.6 1.0 %collective-permute-done.10 = bf16[2,128,256]{2,1,0:T(8,128)(2,1)S(1)} collective-permute-done((bf16[2,128,256]{2,1,0:T(8,128)(2,1)S(1)}, bf16[2,128,256]{2,1,0:T(8,128)(2,1)S(1)}, u32[]{:S(2)}, u32[]{:S(2)}) %collective-permute-start.10) | collective-permute-done | bytes 131104 | tf_op jit(solution)/shard_map/ppermute | solution.py:168
  56.6 2.5 %collective-permute-done.11 = bf16[2,128,256]{2,1,0:T(8,128)(2,1)S(1)} collective-permute-done((bf16[2,128,256]{2,1,0:T(8,128)(2,1)S(1)}, bf16[2,128,256]{2,1,0:T(8,128)(2,1)S(1)}, u32[]{:S(2)}, u32[]{:S(2)}) %collective-permute-start.11) | collective-permute-done | bytes 131104 | tf_op jit(solution)/shard_map/ppermute | solution.py:165
  59.1 2.3 %collective-permute-done.12 = bf16[2,128,256]{2,1,0:T(8,128)(2,1)S(1)} collective-permute-done((bf16[2,128,256]{2,1,0:T(8,128)(2,1)S(1)}, bf16[2,128,256]{2,1,0:T(8,128)(2,1)S(1)}, u32[]{:S(2)}, u32[]{:S(2)}) %collective-permute-start.12) | collective-permute-done | bytes 131104 | tf_op jit(solution)/shard_map/ppermute | solution.py:169
  61.5 0.1 collective-permute-start.13
  61.5 1.3 %collective-permute-done.13 = bf16[2,2,64,256]{3,2,1,0:T(8,128)(2,1)S(1)} collective-permute-done((bf16[2,2,64,256]{3,2,1,0:T(8,128)(2,1)S(1)}, bf16[2,2,64,256]{3,2,1,0:T(8,128)(2,1)S(1)}, u32[]{:S(2)}, u32[]{:S(2)}) %collective-permute-start.13) | collective-permute-done | bytes 131104 | tf_op jit(solution)/shard_map/ppermute | solution.py:165
  63.0 0.1 copy.12
  63.1 0.7 %unstack.15 = bf16[64,8,128]{2,1,0:T(8,128)(2,1)} reshape(bf16[1,64,4,256]{3,2,1,0:T(4,128)(2,1)S(1)} %copy.12) | data formatting | bytes 262144 | tf_op jit(solution)/shard_map/unstack | solution.py:225
  63.8 0.1 copy.11
  63.9 0.7 %unstack.13 = bf16[64,8,128]{2,1,0:T(8,128)(2,1)} reshape(bf16[1,64,4,256]{3,2,1,0:T(4,128)(2,1)S(1)} %copy.11) | data formatting | bytes 262144 | tf_op jit(solution)/shard_map/unstack | solution.py:225
  (36 shorter events, 0.5 us)
Async XLA Ops:
  1.6 0.9 %copy-start.3 = (bf16[64,8,128]{2,1,0:T(8,128)(2,1)S(1)}, bf16[64,8,128]{2,1,0:T(8,128)(2,1)}, u32[]{:S(2)}) copy-start(bf16[64,8,128]{2,1,0:T(8,128)(2,1)} %param.7) | copy-start | bytes 393220
  2.7 1.5 %collective-permute-start = (bf16[2,2,64,256]{3,2,1,0:T(8,128)(2,1)S(1)}, bf16[2,2,64,256]{3,2,1,0:T(8,128)(2,1)S(1)}, u32[]{:S(2)}, u32[]{:S(2)}) collective-permute-start(bf16[2,2,64,256]{3,2,1,0:T(8,128)(2,1)S(1)} %pad_maximum_fusion.2), channel_id=1, source_target_pairs={{0,1},{1,0},{2,3},{3,2},{4,5},{5,4},{6,7},{7,6},{8,9},{9,8},{10,11... | collective-permute-start | bytes 393224 | tf_op jit(solution)/shard_map/ppermute | solution.py:165
  4.3 9.2 %collective-permute-start.2 = (bf16[2,128,256]{2,1,0:T(8,128)(2,1)S(1)}, bf16[2,128,256]{2,1,0:T(8,128)(2,1)S(1)}, u32[]{:S(2)}, u32[]{:S(2)}) collective-permute-start(bf16[2,128,256]{2,1,0:T(8,128)(2,1)S(1)} %pad_maximum_fusion.4), channel_id=1, source_target_pairs={{0,4},{4,0},{8,12},{12,8},{16,20},{20,16},{24,28},{28,24},{1,5},{5... | collective-permute-start | bytes 393224 | tf_op jit(solution)/shard_map/ppermute | solution.py:168
  7.2 7.9 %collective-permute-start.3 = (bf16[2,128,256]{2,1,0:T(8,128)(2,1)S(1)}, bf16[2,128,256]{2,1,0:T(8,128)(2,1)S(1)}, u32[]{:S(2)}, u32[]{:S(2)}) collective-permute-start(bf16[2,128,256]{2,1,0:T(8,128)(2,1)S(1)} %pad_maximum_fusion.3), channel_id=1, source_target_pairs={{0,6},{1,7},{2,4},{3,5},{4,2},{5,3},{6,0},{7,1},{8,14},{9,15},{10,... | collective-permute-start | bytes 393224 | tf_op jit(solution)/shard_map/ppermute | solution.py:169
  8.8 11.2 %collective-permute-start.5 = (bf16[2,128,256]{2,1,0:T(8,128)(2,1)S(1)}, bf16[2,128,256]{2,1,0:T(8,128)(2,1)S(1)}, u32[]{:S(2)}, u32[]{:S(2)}) collective-permute-start(bf16[2,128,256]{2,1,0:T(8,128)(2,1)S(1)} %pad_maximum_fusion.4), channel_id=1, source_target_pairs={{0,8},{4,12},{8,16},{12,20},{16,24},{20,28},{24,0},{28,4},{1,9},{5... | collective-permute-start | bytes 393224 | tf_op jit(solution)/shard_map/ppermute | solution.py:168
  10.4 9.6 %collective-permute-start.6 = (bf16[2,128,256]{2,1,0:T(8,128)(2,1)S(1)}, bf16[2,128,256]{2,1,0:T(8,128)(2,1)S(1)}, u32[]{:S(2)}, u32[]{:S(2)}) collective-permute-start(bf16[2,128,256]{2,1,0:T(8,128)(2,1)S(1)} %pad_maximum_fusion.3), channel_id=1, source_target_pairs={{0,10},{1,11},{2,8},{3,9},{4,14},{5,15},{6,12},{7,13},{8,18},{9,19... | collective-permute-start | bytes 393224 | tf_op jit(solution)/shard_map/ppermute | solution.py:169
  11.9 8.7 %collective-permute-start.1 = (bf16[2,128,256]{2,1,0:T(8,128)(2,1)S(1)}, bf16[2,128,256]{2,1,0:T(8,128)(2,1)S(1)}, u32[]{:S(2)}, u32[]{:S(2)}) collective-permute-start(bf16[2,128,256]{2,1,0:T(8,128)(2,1)S(1)} %pad_maximum_fusion.3), channel_id=1, source_target_pairs={{0,2},{1,3},{2,0},{3,1},{4,6},{5,7},{6,4},{7,5},{8,10},{9,11},{10,... | collective-permute-start | bytes 393224 | tf_op jit(solution)/shard_map/ppermute | solution.py:165
  13.4 15.7 %copy-start.2 = (s32[8]{0:T(128)S(1)}, s32[8]{0:T(128)}, u32[]{:S(2)}) copy-start(s32[8]{0:T(128)} %lengths_ref.1) | copy-start | bytes 100
  13.5 15.7 %copy-start = (bf16[256,16,128]{2,1,0:T(8,128)(2,1)S(1)}, bf16[256,16,128]{2,1,0:T(8,128)(2,1)}, u32[]{:S(2)}) copy-start(bf16[256,16,128]{2,1,0:T(8,128)(2,1)} %q_ref.1) | copy-start | bytes 3145732
  13.5 15.7 %copy-start.1 = (bf16[256,16,128]{2,1,0:T(8,128)(2,1)S(1)}, bf16[256,16,128]{2,1,0:T(8,128)(2,1)}, u32[]{:S(2)}) copy-start(bf16[256,16,128]{2,1,0:T(8,128)(2,1)} %g_ref.1) | copy-start | bytes 3145732
  15.1 8.7 %collective-permute-start.4 = (bf16[2,256,256]{2,1,0:T(8,128)(2,1)S(1)}, bf16[2,256,256]{2,1,0:T(8,128)(2,1)S(1)}, u32[]{:S(2)}, u32[]{:S(2)}) collective-permute-start(bf16[2,256,256]{2,1,0:T(8,128)(2,1)S(1)} %constant_dynamic-update-slice_fusion), channel_id=1, source_target_pairs={{0,8},{8,16},{16,24},{1,9},{9,17},{17,25},{2,10},{10,18},{18,26},{... | collective-permute-start | bytes 786440 | tf_op jit(solution)/shard_map/ppermute | solution.py:174
  20.1 9.1 %collective-permute-start.7 = (bf16[2,256,256]{2,1,0:T(8,128)(2,1)S(1)}, bf16[2,256,256]{2,1,0:T(8,128)(2,1)S(1)}, u32[]{:S(2)}, u32[]{:S(2)}) collective-permute-start(bf16[2,256,256]{2,1,0:T(8,128)(2,1)S(1)} %constant_dynamic-update-slice_fusion.2.refs_2_), channel_id=1, source_target_pairs={{0,4},{4,8},{8,12},{12,16},{16,20},{20,24},{24,28},{28,0},{1,5},{5... | collective-permute-start | bytes 786440 | tf_op jit(solution)/shard_map/ppermute | solution.py:168
  34.8 9.4 %collective-permute-start.8 = (bf16[2,256,256]{2,1,0:T(8,128)(2,1)S(1)}, bf16[2,256,256]{2,1,0:T(8,128)(2,1)S(1)}, u32[]{:S(2)}, u32[]{:S(2)}) collective-permute-start(bf16[2,256,256]{2,1,0:T(8,128)(2,1)S(1)} %get-tuple-element.13), channel_id=1, source_target_pairs={{0,4},{4,0},{8,12},{12,8},{16,20},{20,16},{24,28},{28,24},{1,5},{5... | collective-permute-start | bytes 786440 | tf_op jit(solution)/shard_map/ppermute | solution.py:168
  34.8 13.2 %collective-permute-start.9 = (bf16[2,256,256]{2,1,0:T(8,128)(2,1)S(1)}, bf16[2,256,256]{2,1,0:T(8,128)(2,1)S(1)}, u32[]{:S(2)}, u32[]{:S(2)}) collective-permute-start(bf16[2,256,256]{2,1,0:T(8,128)(2,1)S(1)} %get-tuple-element.15), channel_id=1, source_target_pairs={{0,28},{4,0},{8,4},{12,8},{16,12},{20,16},{24,20},{28,24},{1,29},{... | collective-permute-start | bytes 786440 | tf_op jit(solution)/shard_map/ppermute | solution.py:168
  48.2 8.3 %collective-permute-start.10 = (bf16[2,128,256]{2,1,0:T(8,128)(2,1)S(1)}, bf16[2,128,256]{2,1,0:T(8,128)(2,1)S(1)}, u32[]{:S(2)}, u32[]{:S(2)}) collective-permute-start(bf16[2,128,256]{2,1,0:T(8,128)(2,1)S(1)} %get-tuple-element.22), channel_id=1, source_target_pairs={{0,24},{4,28},{8,0},{12,4},{16,8},{20,12},{24,16},{28,20},{1,25},{... | collective-permute-start | bytes 393224 | tf_op jit(solution)/shard_map/ppermute | solution.py:168
  54.1 5.0 %collective-permute-start.11 = (bf16[2,128,256]{2,1,0:T(8,128)(2,1)S(1)}, bf16[2,128,256]{2,1,0:T(8,128)(2,1)S(1)}, u32[]{:S(2)}, u32[]{:S(2)}) collective-permute-start(bf16[2,128,256]{2,1,0:T(8,128)(2,1)S(1)} %slice.177), channel_id=1, source_target_pairs={{0,2},{1,3},{2,0},{3,1},{4,6},{5,7},{6,4},{7,5},{8,10},{9,11},{10,... | collective-permute-start | bytes 393224 | tf_op jit(solution)/shard_map/ppermute | solution.py:165
  55.5 5.9 %collective-permute-start.12 = (bf16[2,128,256]{2,1,0:T(8,128)(2,1)S(1)}, bf16[2,128,256]{2,1,0:T(8,128)(2,1)S(1)}, u32[]{:S(2)}, u32[]{:S(2)}) collective-permute-start(bf16[2,128,256]{2,1,0:T(8,128)(2,1)S(1)} %get-tuple-element.23), channel_id=1, source_target_pairs={{0,26},{1,27},{2,24},{3,25},{4,30},{5,31},{6,28},{7,29},{8,2},{9,3... | collective-permute-start | bytes 393224 | tf_op jit(solution)/shard_map/ppermute | solution.py:169
  61.5 1.4 %collective-permute-start.13 = (bf16[2,2,64,256]{3,2,1,0:T(8,128)(2,1)S(1)}, bf16[2,2,64,256]{3,2,1,0:T(8,128)(2,1)S(1)}, u32[]{:S(2)}, u32[]{:S(2)}) collective-permute-start(bf16[2,2,64,256]{3,2,1,0:T(8,128)(2,1)S(1)} %pad_maximum_fusion.5), channel_id=1, source_target_pairs={{0,1},{1,0},{2,3},{3,2},{4,5},{5,4},{6,7},{7,6},{8,9},{9,8},{10,11... | collective-permute-start | bytes 393224 | tf_op jit(solution)/shard_map/ppermute | solution.py:165
